TPU v7x, 32 devices: a whole 2x2x4 slice. The times are simulated.
32 devices in a mesh: cells: 8 (over z, x), rhs: 4 (over y, core).
Axes of the slice: x: 2, y: 2, z: 4, core: 2. Of those that a mesh axis runs over, the one named last changes fastest.
Arguments:
- right_side: bfloat16 [64, 512, 384], P('cells', 'rhs'), may hold values from -6 to 6
- leaf_inverse: bfloat16 [64, 384, 384], P('cells'), may hold values from -0.3125 to 0.3125
- leaf_couple: bfloat16 [64, 9, 384, 128], P('cells'), may hold values from -0.3125 to 0.3125
- skel_target: int32 [64, 9], P('cells'), may hold values from 0 to 255, as said below
- skeleton_in: float32 [512, 256, 128], P('rhs', 'cells'), may hold values from -6 to 6
- lift_ops: bfloat16 [8, 4096, 512], P('cells', None, 'rhs'), may hold values from -0.09375 to 0.09375
- node_mix: bfloat16 [8, 1024, 512], P('cells', None, 'rhs'), may hold values from -0.1875 to 0.1875
- node_couple: bfloat16 [8, 512, 512], P('cells', None, 'rhs'), may hold values from -0.125 to 0.125
Outputs:
- leaf_solution: bfloat16 [64, 512, 384], P('cells', 'rhs')
- skeleton_rhs: float32 [512, 256, 128], P('rhs', 'cells')
- node_solution: bfloat16 [8, 512, 512], P('cells', 'rhs')
- node_skeleton: float32 [8, 512, 512], P('cells', 'rhs')
Inputs may be any that keep to these rules, and one draw needn't show every extreme that they name: `skel_target`: entry (c, k) names a skeleton block; its owner device, the entry // 32, lies at most 2 positions along cells from the cell's device c // 8, and on every device some slot reaches that distance.
All inputs are finite; a program needn't handle non-finite values.
Results may differ from a plain program's by a relative error of at most 0.03.
Values may be sent and summed in bfloat16 or wider, within the bound.
A program may use at most 128 MiB of HBM per device.

v0:
```python
import jax
import jax.numpy as jnp
from jax import lax
from jax.sharding import PartitionSpec as P

HOP = 2


def passed_along(value, axis, steps):
    count = lax.axis_size(axis)
    initial, last = (max(0, -steps), min(count, count - steps))
    return lax.ppermute(value, axis, [(source, source + steps) for source in range(initial, last)])


def passed_along_2(value, axis, by):
    devices = lax.axis_size(axis)
    return lax.ppermute(value, axis, [(i, (i + by) % devices) for i in range(devices)])


def on_device(
    right_side, leaf_inverse, leaf_couple, skel_target, skeleton_in, lift_ops, node_mix, node_couple
):
    position = lax.axis_index("cells")
    total_devices = lax.axis_size("cells")
    levels = total_devices.bit_length() - 1
    columns = right_side.shape[1]
    blocks = skeleton_in.shape[1]
    block_width = skeleton_in.shape[2]
    solved = jnp.einsum(
        "ncr,nrq->ncq", right_side, leaf_inverse, preferred_element_type=jnp.float32
    ).astype(jnp.bfloat16)
    updates = jnp.einsum("ncr,nkrs->nkcs", solved, leaf_couple, preferred_element_type=jnp.float32)
    slot_count = updates.shape[0] * updates.shape[1]
    updates = updates.reshape(slot_count, columns, block_width)
    targets = skel_target.reshape(slot_count)
    owners = targets // blocks
    within = targets % blocks
    offsets = owners - position
    hop_reach = HOP
    span_rows = 2 * hop_reach + 1
    segment_ids = (offsets + hop_reach) * blocks + within
    summed = jax.ops.segment_sum(updates, segment_ids, num_segments=span_rows * blocks)
    portions = jnp.transpose(summed.reshape(span_rows, blocks, columns, block_width), (0, 2, 1, 3))
    arrived = portions[hop_reach]
    for distance in list(range(-hop_reach, 0)) + list(range(1, hop_reach + 1)):
        arrived = arrived + passed_along(
            portions[hop_reach + distance].astype(jnp.bfloat16), "cells", distance
        ).astype(jnp.float32)
    skeleton_rhs = skeleton_in - arrived
    gathered = (
        lax.all_gather(lift_ops[0], "rhs", axis=1, tiled=True),
        lax.all_gather(node_mix[0], "rhs", axis=1, tiled=True),
        lax.all_gather(node_couple[0], "rhs", axis=1, tiled=True),
    )

    def multiply(operand, which_op):
        return jnp.dot(operand, gathered[which_op], preferred_element_type=jnp.float32)

    def merge_node(left_child, right_child):
        joined = jnp.concatenate([left_child, right_child], axis=1)
        solution = multiply(joined, 1).astype(jnp.bfloat16)
        skeleton = 0.5 * (
            left_child.astype(jnp.float32) + right_child.astype(jnp.float32)
        ) - multiply(solution, 2)
        return (solution, skeleton)

    flattened = skeleton_rhs.reshape(columns, blocks * block_width).astype(jnp.bfloat16)
    current = multiply(flattened, 0).astype(jnp.bfloat16)
    level_solution = jnp.zeros_like(current)
    for section_level in range(1, levels + 1):
        distance = max(1, 2 ** (section_level - 2))
        left_child = passed_along_2(current, "cells", distance)
        if section_level == 1:
            right_child = current
        else:
            right_child = passed_along_2(current, "cells", -distance)
        level_solution, skeleton = merge_node(left_child, right_child)
        current = skeleton.astype(jnp.bfloat16)
    root_pair = passed_along_2(jnp.stack([current, level_solution]), "cells", -(total_devices // 2))
    node_solution, node_skeleton = merge_node(root_pair[0], root_pair[1])
    return (solved, skeleton_rhs, node_solution[None], node_skeleton[None])


def solution(mesh):
    return jax.shard_map(
        on_device,
        mesh=mesh,
        in_specs=(
            P("cells", "rhs", None),
            P("cells", None, None),
            P("cells", None, None, None),
            P("cells", None),
            P("rhs", "cells", None),
            P("cells", None, "rhs"),
            P("cells", None, "rhs"),
            P("cells", None, "rhs"),
        ),
        out_specs=(
            P("cells", "rhs", None),
            P("rhs", "cells", None),
            P("cells", "rhs", None),
            P("cells", "rhs", None),
        ),
        check_vma=False,
    )
```

profile of v0, /device:TPU:0, one launch (start us, length us, event | category | flops | bytes accessed | tf_op | source)
XLA Modules:
  0.0 172.8 jit_solution(12995412638353398102)
XLA Ops:
  8.8 1.8 %convolution_convert_fusion = bf16[8,128,384]{2,1,0:T(8,128)(2,1)S(1)} fusion(bf16[8,128,384]{2,1,0:T(8,128)(2,1)} %param.8, bf16[8,384,384]{2,1,0:T(8,128)(2,1)S(1)} %copy-done), kind=kOutput, calls=%fused_computation.9 | convolution fusion | flops 302383104 | bytes 3932160 | tf_op jit(solution)/shard_map/ncr,nrq->ncq/dot_general | solution.py:29
  10.7 7.0 %fusion.18 = f32[8,128,9,128]{3,1,2,0:T(8,128)} fusion(bf16[8,9,384,128]{3,2,1,0:T(8,128)(2,1)} %param.10, bf16[8,128,384]{2,1,0:T(8,128)(2,1)S(1)} %convolution_convert_fusion), kind=kOutput, calls=%fused_computation.25 | convolution fusion | flops 905969664 | bytes 12582912 | tf_op jit(solution)/shard_map/ncr,nkrs->nkcs/dot_general | solution.py:32
  17.7 5.6 %broadcast_in_dim.10 = f32[160,128,128]{2,1,0:T(8,128)} broadcast(f32[]{:T(128)} %constant.30.clone.1), dimensions={} | broadcast | bytes 10485764 | tf_op jit(solution)/shard_map/broadcast_in_dim | solution.py:42
  23.3 16.6 %scatter_fusion = f32[160,128,128]{2,1,0:T(8,128)} fusion(f32[160,128,128]{2,1,0:T(8,128)} %broadcast_in_dim.10, s32[72]{0:T(128)S(1)} %fusion.46, f32[72,128,128]{2,1,0:T(8,128)} %bitcast.94), kind=kCustom, calls=%fused_computation | custom fusion | flops 1179648 | bytes 14156064 | tf_op jit(solution)/shard_map/scatter-add | solution.py:42
  39.8 5.3 %convert.6 = bf16[5,128,32,128]{3,1,2,0:T(8,128)(2,1)S(1)} convert(f32[5,128,32,128]{3,1,2,0:T(8,128)} %bitcast.92) | non-fusion elementwise | flops 2621440 | bytes 15728640 | tf_op jit(solution)/shard_map/convert.3
  45.1 2.1 %slice_bitcast_fusion.4 = (bf16[128,32,128]{2,0,1:T(8,128)(2,1)}, bf16[128,32,128]{2,0,1:T(8,128)(2,1)}, bf16[128,32,128]{2,0,1:T(8,128)(2,1)}, bf16[128,32,128]{2,0,1:T(8,128)(2,1)}) fusion(bf16[5,128,32,128]{3,1,2,0:T(8,128)(2,1)S(1)} %convert.6), kind=kLoop, calls=%fused_computation.20 | loop fusion | bytes 8388608 | tf_op jit(solution)/shard_map/convert_element_type | solution.py:47
  49.8 6.5 %collective-permute-start.2 = (bf16[128,32,128]{2,0,1:T(8,128)(2,1)}, bf16[128,32,128]{2,0,1:T(8,128)(2,1)}, u32[]{:S(2)}, u32[]{:S(2)}) collective-permute-start(bf16[128,32,128]{2,0,1:T(8,128)(2,1)} %get-tuple-element.16), channel_id=1, source_target_pairs={{0,4},{4,8},{8,12},{12,16},{16,20},{20,24},{24,28},{1,5},{5,9},{9,... | collective-permute-start | bytes 3145736 | tf_op jit(solution)/shard_map/ppermute | solution.py:12
  56.3 4.6 %collective-permute-start.3 = (bf16[128,32,128]{2,0,1:T(8,128)(2,1)}, bf16[128,32,128]{2,0,1:T(8,128)(2,1)}, u32[]{:S(2)}, u32[]{:S(2)}) collective-permute-start(bf16[128,32,128]{2,0,1:T(8,128)(2,1)} %get-tuple-element.15), channel_id=1, source_target_pairs={{0,8},{4,12},{8,16},{12,20},{16,24},{20,28},{1,9},{5,13},{9,17},{1... | collective-permute-start | bytes 3145736 | tf_op jit(solution)/shard_map/ppermute | solution.py:12
  61.0 15.4 %collective-permute-done = bf16[128,32,128]{2,0,1:T(8,128)(2,1)S(1)} collective-permute-done((bf16[128,32,128]{2,0,1:T(8,128)(2,1)}, bf16[128,32,128]{2,0,1:T(8,128)(2,1)S(1)}, u32[]{:S(2)}, u32[]{:S(2)}) %collective-permute-start) | collective-permute-done | bytes 1048608 | tf_op jit(solution)/shard_map/ppermute | solution.py:12
  76.9 23.7 %collective-permute-done.2 = bf16[128,32,128]{2,0,1:T(8,128)(2,1)} collective-permute-done((bf16[128,32,128]{2,0,1:T(8,128)(2,1)}, bf16[128,32,128]{2,0,1:T(8,128)(2,1)}, u32[]{:S(2)}, u32[]{:S(2)}) %collective-permute-start.2) | collective-permute-done | bytes 1048608 | tf_op jit(solution)/shard_map/ppermute | solution.py:12
  100.5 6.6 %fusion.65 = (bf16[128,32,128]{2,0,1:T(8,128)(2,1)}, f32[128,32,128]{2,0,1:T(8,128)}) fusion(bf16[128,32,128]{2,0,1:T(8,128)(2,1)} %collective-permute-done.3, bf16[128,32,128]{2,0,1:T(8,128)(2,1)} %collective-permute-done.2, bf16[128,32,128]{2,0,1:T(8,128)(2,1)} %collective-permute-done.1, bf16[128,32,128]{2,0,1:T(8,128)(2,1)S(1)} %collective-permute-done, ...), kind=kLoop, calls=%fused_computation.64 | loop fusion | flops 5242880 | bytes 11534336 | tf_op jit(solution)/shard_map/convert_element_type | solution.py:67
  108.7 2.9 %fusion.7 = bf16[128,512]{1,0:T(8,128)(2,1)S(1)} fusion(bf16[128,4096]{0,1:T(8,128)(2,1)S(1)} %bitcast.95, bf16[1,4096,512]{2,1,0:T(8,128)(2,1)} %all-gather.6.cloned.1.call-done), kind=kOutput, calls=%fused_computation.10 | convolution fusion | flops 536936448 | bytes 5373952 | tf_op jit(solution)/shard_map/dot_general | solution.py:57
  111.7 2.7 %collective-permute-start.4 = (bf16[128,512]{1,0:T(8,128)(2,1)S(1)}, bf16[128,512]{1,0:T(8,128)(2,1)}, u32[]{:S(2)}, u32[]{:S(2)}) collective-permute-start(bf16[128,512]{1,0:T(8,128)(2,1)S(1)} %fusion.7), channel_id=1, source_target_pairs={{0,4},{4,8},{8,12},{12,16},{16,20},{20,24},{24,28},{28,0},{1,5},{5... | collective-permute-start | bytes 393224 | tf_op jit(solution)/shard_map/ppermute | solution.py:17
  114.4 8.3 %all-gather.2 = bf16[1,512,512]{2,1,0:T(8,128)(2,1)} all-gather(bf16[1,512,128]{2,1,0:T(8,128)(2,1)} %param.15), channel_id=4, replica_groups=mesh['cells'=8,'rhs'=4] {'rhs'}, dimensions={2}, use_global_device_ids=true | all-gather | bytes 655360 | tf_op jit(solution)/shard_map/all_gather | solution.py:53
  122.7 2.7 %subtract_convert_fusion.2 = bf16[128,512]{1,0:T(8,128)(2,1)} fusion(bf16[128,512]{1,0:T(8,128)(2,1)S(1)} %fusion.7, bf16[128,512]{1,0:T(8,128)(2,1)} %collective-permute-done.4, bf16[1,512,512]{2,1,0:T(8,128)(2,1)} %all-gather.2, bf16[1,1024,512]{2,1,0:T(8,128)(2,1)} %all-gather.8.cloned.1.call-done), kind=kOutput, calls=%fused_computation.49 | convolution fusion | flops 202309632 | bytes 1966080 | tf_op jit(solution)/shard_map/dot_general | solution.py:57
  126.7 3.4 %collective-permute-start.6 = (bf16[128,512]{1,0:T(8,128)(2,1)}, bf16[128,512]{1,0:T(8,128)(2,1)}, u32[]{:S(2)}, u32[]{:S(2)}) collective-permute-start(bf16[128,512]{1,0:T(8,128)(2,1)} %subtract_convert_fusion.2), channel_id=1, source_target_pairs={{0,28},{4,0},{8,4},{12,8},{16,12},{20,16},{24,20},{28,24},{1,29},{... | collective-permute-start | bytes 393224 | tf_op jit(solution)/shard_map/ppermute | solution.py:17
  130.1 4.3 %collective-permute-done.5 = bf16[128,512]{1,0:T(8,128)(2,1)S(1)} collective-permute-done((bf16[128,512]{1,0:T(8,128)(2,1)}, bf16[128,512]{1,0:T(8,128)(2,1)S(1)}, u32[]{:S(2)}, u32[]{:S(2)}) %collective-permute-start.5) | collective-permute-done | bytes 131104 | tf_op jit(solution)/shard_map/ppermute | solution.py:17
  134.4 1.7 collective-permute-done.6
  136.1 2.6 %subtract_convert_fusion.1 = bf16[128,512]{1,0:T(8,128)(2,1)} fusion(bf16[128,512]{1,0:T(8,128)(2,1)} %collective-permute-done.6, bf16[128,512]{1,0:T(8,128)(2,1)S(1)} %collective-permute-done.5, bf16[1,512,512]{2,1,0:T(8,128)(2,1)} %all-gather.2, bf16[1,1024,512]{2,1,0:T(8,128)(2,1)} %all-gather.8.cloned.1.call-done), kind=kOutput, calls=%fused_computation.48 | convolution fusion | flops 202309632 | bytes 1966080 | tf_op jit(solution)/shard_map/dot_general | solution.py:57
  140.1 2.4 %collective-permute-start.8 = (bf16[128,512]{1,0:T(8,128)(2,1)}, bf16[128,512]{1,0:T(8,128)(2,1)S(1)}, u32[]{:S(2)}, u32[]{:S(2)}) collective-permute-start(bf16[128,512]{1,0:T(8,128)(2,1)} %subtract_convert_fusion.1), channel_id=1, source_target_pairs={{0,24},{4,28},{8,0},{12,4},{16,8},{20,12},{24,16},{28,20},{1,25},{... | collective-permute-start | bytes 393224 | tf_op jit(solution)/shard_map/ppermute | solution.py:17
  142.5 4.6 %collective-permute-done.7 = bf16[128,512]{1,0:T(8,128)(2,1)S(1)} collective-permute-done((bf16[128,512]{1,0:T(8,128)(2,1)}, bf16[128,512]{1,0:T(8,128)(2,1)S(1)}, u32[]{:S(2)}, u32[]{:S(2)}) %collective-permute-start.7) | collective-permute-done | bytes 131104 | tf_op jit(solution)/shard_map/ppermute | solution.py:17
  150.1 2.0 %collective-permute-start.9 = (bf16[2,128,512]{2,1,0:T(8,128)(2,1)S(1)}, bf16[2,128,512]{2,1,0:T(8,128)(2,1)S(1)}, u32[]{:S(2)}, u32[]{:S(2)}) collective-permute-start(bf16[2,128,512]{2,1,0:T(8,128)(2,1)S(1)} %pad_maximum_fusion), channel_id=1, source_target_pairs={{0,16},{4,20},{8,24},{12,28},{16,0},{20,4},{24,8},{28,12},{1,17},{... | collective-permute-start | bytes 786440 | tf_op jit(solution)/shard_map/ppermute | solution.py:17
  152.2 2.5 %copy.16 = f32[128,32,128]{2,1,0:T(8,128)} copy(f32[128,32,128]{2,0,1:T(8,128)S(1)} %copy-done.3) | data formatting | bytes 4194304
  154.7 9.9 %collective-permute-done.9 = bf16[2,128,512]{2,1,0:T(8,128)(2,1)S(1)} collective-permute-done((bf16[2,128,512]{2,1,0:T(8,128)(2,1)S(1)}, bf16[2,128,512]{2,1,0:T(8,128)(2,1)S(1)}, u32[]{:S(2)}, u32[]{:S(2)}) %collective-permute-start.9) | collective-permute-done | bytes 262176 | tf_op jit(solution)/shard_map/ppermute | solution.py:17
  (35 shorter events, 13.4 us)
Async XLA Ops:
  7.2 1.7 copy-start
  7.2 101.5 %all-gather.6.cloned.1.call-start = ((), (), s32[]{:S(2)}) async-start(), calls=%async_computation | async-start | bytes 5242880 | tf_op jit(solution)/shard_map/all_gather | solution.py:51
  7.9 114.8 %all-gather.8.cloned.1.call-start = ((), (), s32[]{:S(2)}) async-start(), calls=%async_computation.1 | async-start | bytes 1310720 | tf_op jit(solution)/shard_map/all_gather | solution.py:52
  10.7 7.0 %copy-start.4 = (bf16[8,128,384]{2,1,0:T(8,128)(2,1)}, bf16[8,128,384]{2,1,0:T(8,128)(2,1)S(1)}, u32[]{:S(2)}) copy-start(bf16[8,128,384]{2,1,0:T(8,128)(2,1)S(1)} %convolution_convert_fusion) | copy-start | bytes 2359300
  47.2 29.2 %collective-permute-start = (bf16[128,32,128]{2,0,1:T(8,128)(2,1)}, bf16[128,32,128]{2,0,1:T(8,128)(2,1)S(1)}, u32[]{:S(2)}, u32[]{:S(2)}) collective-permute-start(bf16[128,32,128]{2,0,1:T(8,128)(2,1)} %get-tuple-element.14), channel_id=1, source_target_pairs={{8,0},{12,4},{16,8},{20,12},{24,16},{28,20},{9,1},{13,5},{17,9},{2... | collective-permute-start | bytes 3145736 | tf_op jit(solution)/shard_map/ppermute | solution.py:12
  48.5 28.4 %collective-permute-start.1 = (bf16[128,32,128]{2,0,1:T(8,128)(2,1)}, bf16[128,32,128]{2,0,1:T(8,128)(2,1)}, u32[]{:S(2)}, u32[]{:S(2)}) collective-permute-start(bf16[128,32,128]{2,0,1:T(8,128)(2,1)} %get-tuple-element.17), channel_id=1, source_target_pairs={{4,0},{8,4},{12,8},{16,12},{20,16},{24,20},{28,24},{5,1},{9,5},{13... | collective-permute-start | bytes 3145736 | tf_op jit(solution)/shard_map/ppermute | solution.py:12
  49.8 50.7 %collective-permute-start.2 = (bf16[128,32,128]{2,0,1:T(8,128)(2,1)}, bf16[128,32,128]{2,0,1:T(8,128)(2,1)}, u32[]{:S(2)}, u32[]{:S(2)}) collective-permute-start(bf16[128,32,128]{2,0,1:T(8,128)(2,1)} %get-tuple-element.16), channel_id=1, source_target_pairs={{0,4},{4,8},{8,12},{12,16},{16,20},{20,24},{24,28},{1,5},{5,9},{9,... | collective-permute-start | bytes 3145736 | tf_op jit(solution)/shard_map/ppermute | solution.py:12
  56.3 44.2 %collective-permute-start.3 = (bf16[128,32,128]{2,0,1:T(8,128)(2,1)}, bf16[128,32,128]{2,0,1:T(8,128)(2,1)}, u32[]{:S(2)}, u32[]{:S(2)}) collective-permute-start(bf16[128,32,128]{2,0,1:T(8,128)(2,1)} %get-tuple-element.15), channel_id=1, source_target_pairs={{0,8},{4,12},{8,16},{12,20},{16,24},{20,28},{1,9},{5,13},{9,17},{1... | collective-permute-start | bytes 3145736 | tf_op jit(solution)/shard_map/ppermute | solution.py:12
  111.7 11.0 %collective-permute-start.4 = (bf16[128,512]{1,0:T(8,128)(2,1)S(1)}, bf16[128,512]{1,0:T(8,128)(2,1)}, u32[]{:S(2)}, u32[]{:S(2)}) collective-permute-start(bf16[128,512]{1,0:T(8,128)(2,1)S(1)} %fusion.7), channel_id=1, source_target_pairs={{0,4},{4,8},{8,12},{12,16},{16,20},{20,24},{24,28},{28,0},{1,5},{5... | collective-permute-start | bytes 393224 | tf_op jit(solution)/shard_map/ppermute | solution.py:17
  122.7 25.7 %copy-start.1 = (bf16[1,1024,512]{2,1,0:T(8,128)(2,1)S(1)}, bf16[1,1024,512]{2,1,0:T(8,128)(2,1)}, u32[]{:S(2)}) copy-start(bf16[1,1024,512]{2,1,0:T(8,128)(2,1)} %all-gather.8.cloned.1.call-done) | copy-start | bytes 3145732
  125.4 9.1 %collective-permute-start.5 = (bf16[128,512]{1,0:T(8,128)(2,1)}, bf16[128,512]{1,0:T(8,128)(2,1)S(1)}, u32[]{:S(2)}, u32[]{:S(2)}) collective-permute-start(bf16[128,512]{1,0:T(8,128)(2,1)} %subtract_convert_fusion.2), channel_id=1, source_target_pairs={{0,4},{4,8},{8,12},{12,16},{16,20},{20,24},{24,28},{28,0},{1,5},{5... | collective-permute-start | bytes 393224 | tf_op jit(solution)/shard_map/ppermute | solution.py:17
  126.7 9.4 %collective-permute-start.6 = (bf16[128,512]{1,0:T(8,128)(2,1)}, bf16[128,512]{1,0:T(8,128)(2,1)}, u32[]{:S(2)}, u32[]{:S(2)}) collective-permute-start(bf16[128,512]{1,0:T(8,128)(2,1)} %subtract_convert_fusion.2), channel_id=1, source_target_pairs={{0,28},{4,0},{8,4},{12,8},{16,12},{20,16},{24,20},{28,24},{1,29},{... | collective-permute-start | bytes 393224 | tf_op jit(solution)/shard_map/ppermute | solution.py:17
  138.7 13.5 %copy-start.3 = (f32[128,32,128]{2,0,1:T(8,128)S(1)}, f32[128,32,128]{2,0,1:T(8,128)}, u32[]{:S(2)}) copy-start(f32[128,32,128]{2,0,1:T(8,128)} %get-tuple-element.13) | copy-start | bytes 6291460
  138.7 8.5 %collective-permute-start.7 = (bf16[128,512]{1,0:T(8,128)(2,1)}, bf16[128,512]{1,0:T(8,128)(2,1)S(1)}, u32[]{:S(2)}, u32[]{:S(2)}) collective-permute-start(bf16[128,512]{1,0:T(8,128)(2,1)} %subtract_convert_fusion.1), channel_id=1, source_target_pairs={{0,8},{4,12},{8,16},{12,20},{16,24},{20,28},{24,0},{28,4},{1,9},{5... | collective-permute-start | bytes 393224 | tf_op jit(solution)/shard_map/ppermute | solution.py:17
  140.1 8.3 %collective-permute-start.8 = (bf16[128,512]{1,0:T(8,128)(2,1)}, bf16[128,512]{1,0:T(8,128)(2,1)S(1)}, u32[]{:S(2)}, u32[]{:S(2)}) collective-permute-start(bf16[128,512]{1,0:T(8,128)(2,1)} %subtract_convert_fusion.1), channel_id=1, source_target_pairs={{0,24},{4,28},{8,0},{12,4},{16,8},{20,12},{24,16},{28,20},{1,25},{... | collective-permute-start | bytes 393224 | tf_op jit(solution)/shard_map/ppermute | solution.py:17
  148.8 16.2 %copy-start.2 = (bf16[1,512,512]{2,1,0:T(8,128)(2,1)S(1)}, bf16[1,512,512]{2,1,0:T(8,128)(2,1)}, u32[]{:S(2)}) copy-start(bf16[1,512,512]{2,1,0:T(8,128)(2,1)} %all-gather.2) | copy-start | bytes 1572868
  150.1 14.5 %collective-permute-start.9 = (bf16[2,128,512]{2,1,0:T(8,128)(2,1)S(1)}, bf16[2,128,512]{2,1,0:T(8,128)(2,1)S(1)}, u32[]{:S(2)}, u32[]{:S(2)}) collective-permute-start(bf16[2,128,512]{2,1,0:T(8,128)(2,1)S(1)} %pad_maximum_fusion), channel_id=1, source_target_pairs={{0,16},{4,20},{8,24},{12,28},{16,0},{20,4},{24,8},{28,12},{1,17},{... | collective-permute-start | bytes 786440 | tf_op jit(solution)/shard_map/ppermute | solution.py:17
  165.0 1.0 copy-start.5
Sparse Core Ops, SparseCore 0:
  9.6 37.7 all-gather.5
  61.1 16.6 all-gather.7
where the time goes:
time: 174 us; the launch traced here: 173 us
  waiting for transfers between devices  62.1 us (36%)
  other arithmetic  28.4 us (16%)
  starting transfers between devices  27.1 us (16%)
  matrix products  19.8 us (11%)
  between operations  14.2 us (8%)
  local copies, waits for them, and re-layouts  12.8 us (7%)
  blocking collectives  8.3 us (5%)
    ppermute x4, waiting for transfers between devices, passed_along(): lax.ppermute(value, axis, [(source, source + steps) for source in range(i...  39.5 us
    ppermute x6, waiting for transfers between devices, passed_along_2(): lax.ppermute(value, axis, [(i, (i + by) % devices) for i in range(devices)])  21.8 us
    scatter-add x1, other arithmetic, on_device(): jax.ops.segment_sum(updates, segment_ids, num_segments=span_rows * blocks)  16.6 us
    ppermute x4, starting transfers between devices, passed_along(): lax.ppermute(value, axis, [(source, source + steps) for source in range(i...  13.7 us
    ppermute x6, starting transfers between devices, passed_along_2(): lax.ppermute(value, axis, [(i, (i + by) % devices) for i in range(devices)])  13.3 us
    dot_general x7, matrix products, multiply(): jnp.dot(operand, gathered[which_op], preferred_element_type=jnp.float32)  11 us
    all_gather x1, blocking collectives, on_device(): lax.all_gather(node_couple[0], 'rhs', axis=1, tiled=True)  8.3 us
    dot_general x1, matrix products, on_device(): jnp.einsum('ncr,nkrs->nkcs', solved, leaf_couple, preferred_element_type=...  7 us
  transfers between devices with their start and end apart: 12, of which 8 were waited for; matrix products, arithmetic and copies ran while one was open for 31% of the time, Pallas kernels for 0%

commit v1 on v0

v1 whole, which is shorter than its diff:
```python
import functools

import jax
import jax.numpy as jnp
from jax import lax
from jax.experimental import pallas as pl
from jax.experimental.pallas import tpu as pltpu
from jax.sharding import PartitionSpec as P

HOP = 2
DISTANCES = (-2, -1, 1, 2)
CHUNKS = 4
MESH = pl.DeviceIdType.MESH
F32, BF16 = jnp.float32, jnp.bfloat16


def dot(a, b):
    return jnp.dot(a, b, preferred_element_type=F32)


def leaf_kernel(blocks, slots, seg_ref, x_ref, inv_ref, couple_ref, sol_ref, own_ref, send_ref, acc):
    cell = pl.program_id(0)

    @pl.when(cell == 0)
    def _():
        @pl.loop(0, acc.shape[0])
        def _(i):
            acc[i] = jnp.zeros(acc.shape[1:], F32)

    solved = dot(x_ref[0], inv_ref[0]).astype(BF16)
    sol_ref[0] = solved
    width = couple_ref.shape[-1]
    for k in range(0, slots, 2):
        pair = [j for j in (k, k + 1) if j < slots]
        wide = jnp.concatenate([couple_ref[0, j] for j in pair], axis=1)
        update = dot(solved, wide)
        for at, j in enumerate(pair):
            where = seg_ref[cell * slots + j]
            acc[where] += update[:, at * width : (at + 1) * width]

    @pl.when(cell == pl.num_programs(0) - 1)
    def _():
        for row in range(2 * HOP + 1):
            if row == HOP:
                @pl.loop(0, blocks)
                def _(b):
                    own_ref[b] = acc[row * blocks + b]
            else:
                slot = row if row < HOP else row - 1

                @pl.loop(0, blocks)
                def _(b):
                    send_ref[slot, b] = acc[row * blocks + b].astype(BF16)


def leaf_call(segments, right_side, leaf_inverse, leaf_couple, blocks):
    cells, columns, rw = right_side.shape
    slots, width = leaf_couple.shape[1], leaf_couple.shape[3]
    grid_spec = pltpu.PrefetchScalarGridSpec(
        num_scalar_prefetch=1,
        grid=(cells,),
        in_specs=[
            pl.BlockSpec((1, columns, rw), lambda c, s: (c, 0, 0)),
            pl.BlockSpec((1, rw, rw), lambda c, s: (c, 0, 0)),
            pl.BlockSpec((1, slots, rw, width), lambda c, s: (c, 0, 0, 0)),
        ],
        out_specs=[
            pl.BlockSpec((1, columns, rw), lambda c, s: (c, 0, 0)),
            pl.BlockSpec((blocks, columns, width), lambda c, s: (0, 0, 0)),
            pl.BlockSpec((2 * HOP, blocks, columns, width), lambda c, s: (0, 0, 0, 0)),
        ],
        scratch_shapes=[pltpu.VMEM(((2 * HOP + 1) * blocks, columns, width), F32)],
    )
    return pl.pallas_call(
        functools.partial(leaf_kernel, blocks, slots),
        grid_spec=grid_spec,
        out_shape=[
            jax.ShapeDtypeStruct((cells, columns, rw), BF16),
            jax.ShapeDtypeStruct((blocks, columns, width), F32),
            jax.ShapeDtypeStruct((2 * HOP, blocks, columns, width), BF16),
        ],
        compiler_params=pltpu.CompilerParams(vmem_limit_bytes=48 * 2**20),
    )(segments, right_side, leaf_inverse, leaf_couple)


def tree_kernel(
    n, levels, send, own, skel, lift, mix, couple, out_skel, out_sol, out_node,
    recv, own_v, skel_v, flat, lift_g, mix_g, couple_g, mine, left_v, right_v, sol_v,
    local_sem, port_send, port_recv, near_send, near_recv, far_send, far_recv, fwd_send, fwd_recv,
    vec_send, vec_recv,
):
    me = lax.axis_index("cells")
    rank = lax.axis_index("rhs")
    near = rank + 1 - 2 * (rank % 2)
    far = (rank + 2) % 4
    far_near = (near + 2) % 4
    blocks, columns, width = own_v.shape
    node = couple_g.shape[0]
    reach = [max(1, 2 ** (level - 2)) for level in range(1, levels + 1)]
    partners = sorted({s % n for d in reach + [1, 2, n // 2] for s in (d, -d)})

    barrier = pltpu.get_barrier_semaphore()
    for step in partners:
        pl.semaphore_signal(barrier, inc=1, device_id=((me + step) % n, rank), device_id_type=MESH)
    for other in (near, far):
        pl.semaphore_signal(barrier, inc=1, device_id=(me, other), device_id_type=MESH)
    pl.semaphore_wait(barrier, len(partners) + 2)

    def shard(which):
        return pl.ds(pl.multiple_of(which * width, width), width)

    def remote(src, dst, s_sem, r_sem, cell, at):
        return pltpu.make_async_remote_copy(
            src_ref=src, dst_ref=dst, send_sem=s_sem, recv_sem=r_sem,
            device_id=(cell, at), device_id_type=MESH,
        )

    group = blocks // CHUNKS
    depth = lift.shape[0] // CHUNKS
    pieces = [(lift, lift_g, pl.ds(q * depth, depth)) for q in range(CHUNKS)]
    pieces += [(mix, mix_g, pl.ds(0, mix.shape[0])), (couple, couple_g, pl.ds(0, couple.shape[0]))]

    def to_near(i):
        src, dst, rows = pieces[i]
        return remote(src.at[rows], dst.at[rows, shard(rank)], near_send.at[i], near_recv.at[i], me, near)

    def to_far(i):
        src, dst, rows = pieces[i]
        return remote(src.at[rows], dst.at[rows, shard(rank)], far_send.at[i], far_recv.at[i], me, far)

    def forward(i):
        _, dst, rows = pieces[i]
        place = dst.at[rows, shard(far)]
        return remote(place, place, fwd_send.at[i], fwd_recv.at[i], me, near)

    def near_arrival(i):
        _, dst, rows = pieces[i]
        place = dst.at[rows, shard(near)]
        return remote(place, place, near_send.at[i], near_recv.at[i], me, near)

    def far_arrival(i):
        _, dst, rows = pieces[i]
        place = dst.at[rows, shard(far)]
        return remote(place, place, far_send.at[i], far_recv.at[i], me, far)

    def fwd_arrival(i):
        _, dst, rows = pieces[i]
        place = dst.at[rows, shard(far_near)]
        return remote(place, place, fwd_send.at[i], fwd_recv.at[i], me, near)

    def portion(j, q):
        rows = pl.ds(q * group, group)
        return remote(
            send.at[j, rows], recv.at[j, rows], port_send.at[j, q], port_recv.at[j, q],
            (me + DISTANCES[j] + n) % n, rank,
        )

    def sends_to(j):
        target = me + DISTANCES[j]
        return jnp.logical_and(target >= 0, target < n)

    def hears_from(j):
        source = me - DISTANCES[j]
        return jnp.logical_and(source >= 0, source < n)

    to_far(0).start()
    for q in range(CHUNKS):
        for j in range(len(DISTANCES)):
            @pl.when(sends_to(j))
            def _():
                portion(j, q).start()
        if q == 0:
            for i in range(1, len(pieces)):
                to_far(i).start()
    for i in range(len(pieces)):
        to_near(i).start()
    locals_ = [
        pltpu.make_async_copy(own, own_v, local_sem.at[0]),
        pltpu.make_async_copy(skel, skel_v, local_sem.at[1]),
    ]
    for i, (src, dst, rows) in enumerate(pieces):
        locals_.append(pltpu.make_async_copy(src.at[rows], dst.at[rows, shard(rank)], local_sem.at[2 + i]))
    for copy in locals_:
        copy.start()

    for j in range(len(DISTANCES)):
        @pl.when(jnp.logical_not(hears_from(j)))
        def _():
            @pl.loop(0, blocks)
            def _(b):
                recv[j, b] = jnp.zeros((columns, width), BF16)

    for copy in locals_:
        copy.wait()

    total = None
    for q in range(CHUNKS):
        ready = [q] if q < CHUNKS - 1 else list(range(q, len(pieces)))
        for i in ready:
            far_arrival(i).wait_recv()
            forward(i).start()
        for j in range(len(DISTANCES)):
            @pl.when(hears_from(j))
            def _():
                portion(j, q).wait_recv()
        for b in range(q * group, (q + 1) * group):
            rows = pl.ds(b, columns, stride=blocks)
            arrived = own_v[b]
            for j in range(len(DISTANCES)):
                arrived = arrived + recv[j, b].astype(F32)
            value = skel_v[rows, :] - arrived
            skel_v[rows, :] = value
            flat[:, b * width : (b + 1) * width] = value.astype(BF16)
        near_arrival(q).wait_recv()
        fwd_arrival(q).wait_recv()
        part = dot(flat[:, q * depth : (q + 1) * depth], lift_g[q * depth : (q + 1) * depth, :])
        total = part if total is None else total + part
    mine[0] = total.astype(BF16)

    def vector(src, dst, at, step):
        return remote(src, dst, vec_send.at[at], vec_recv.at[at], (me + step + n) % n, rank)

    result = pltpu.make_async_copy(skel_v, out_skel, local_sem.at[0])
    sent = []

    def merge(first, second):
        solved = (dot(first, mix_g[:node, :]) + dot(second, mix_g[node:, :])).astype(BF16)
        skeleton = 0.5 * (first.astype(F32) + second.astype(F32)) - dot(solved, couple_g[...])
        return solved, skeleton

    solved = None
    for level in range(levels):
        d = reach[level]
        up = vector(mine.at[level], left_v.at[level], 2 * level, d)
        up.start()
        sent.append(up)
        if level > 0:
            down = vector(mine.at[level], right_v.at[level], 2 * level + 1, -d)
            down.start()
            sent.append(down)
        else:
            result.start()
            for i in range(CHUNKS, len(pieces)):
                near_arrival(i).wait_recv()
                fwd_arrival(i).wait_recv()
        up.wait_recv()
        if level > 0:
            down.wait_recv()
            second = right_v[level]
        else:
            second = mine[0]
        solved, skeleton = merge(left_v[level], second)
        if level == levels - 1:
            sol_v[...] = solved
            other = vector(sol_v, right_v.at[0], 2 * levels, n // 2)
            other.start()
        mine[level + 1] = skeleton.astype(BF16)
    up = vector(mine.at[levels], left_v.at[levels], 2 * levels + 1, n // 2)
    up.start()
    sent += [other, up]
    other.wait_recv()
    up.wait_recv()
    solved, skeleton = merge(left_v[levels], right_v[0])
    out_sol[...] = solved
    out_node[...] = skeleton

    for copy in sent:
        copy.wait_send()
    for i in range(len(pieces)):
        to_near(i).wait_send()
        to_far(i).wait_send()
        forward(i).wait_send()
    for j in range(len(DISTANCES)):
        @pl.when(sends_to(j))
        def _():
            for q in range(CHUNKS):
                portion(j, q).wait_send()
    result.wait()


def tree_call(n, send, own, skel, lift, mix, couple):
    blocks, columns, width = own.shape
    node = couple.shape[0]
    levels = n.bit_length() - 1
    pieces = CHUNKS + 2
    dma = pltpu.SemaphoreType.DMA
    vmem = pl.BlockSpec(memory_space=pltpu.VMEM)
    hbm = pl.BlockSpec(memory_space=pl.ANY)
    return pl.pallas_call(
        functools.partial(tree_kernel, n, levels),
        out_shape=[
            jax.ShapeDtypeStruct(skel.shape, F32),
            jax.ShapeDtypeStruct((columns, node), BF16),
            jax.ShapeDtypeStruct((columns, node), F32),
        ],
        in_specs=[hbm] * 6,
        out_specs=[hbm, vmem, vmem],
        scratch_shapes=[
            pltpu.VMEM((2 * HOP, blocks, columns, width), BF16),
            pltpu.VMEM((blocks, columns, width), F32),
            pltpu.VMEM(skel.shape, F32),
            pltpu.VMEM((columns, blocks * width), BF16),
            pltpu.VMEM((lift.shape[0], node), BF16),
            pltpu.VMEM((mix.shape[0], node), BF16),
            pltpu.VMEM((couple.shape[0], node), BF16),
            pltpu.VMEM((levels + 1, columns, node), BF16),
            pltpu.VMEM((levels + 1, columns, node), BF16),
            pltpu.VMEM((levels, columns, node), BF16),
            pltpu.VMEM((columns, node), BF16),
            dma((2 + pieces,)),
            dma((2 * HOP, CHUNKS)),
            dma((2 * HOP, CHUNKS)),
            dma((pieces,)), dma((pieces,)), dma((pieces,)),
            dma((pieces,)), dma((pieces,)), dma((pieces,)),
            dma((2 * levels + 2,)),
            dma((2 * levels + 2,)),
        ],
        compiler_params=pltpu.CompilerParams(
            collective_id=0, has_side_effects=True, vmem_limit_bytes=48 * 2**20
        ),
    )(send, own, skel, lift, mix, couple)


def on_device(
    right_side, leaf_inverse, leaf_couple, skel_target, skeleton_in, lift_ops, node_mix, node_couple
):
    position = lax.axis_index("cells")
    n = lax.axis_size("cells")
    columns, blocks, width = skeleton_in.shape
    segments = skel_target.reshape(-1) - (position - HOP) * blocks
    solved, own, send = leaf_call(segments, right_side, leaf_inverse, leaf_couple, blocks)
    skel, node_solution, node_skeleton = tree_call(
        n, send, own, skeleton_in.reshape(columns * blocks, width),
        lift_ops[0], node_mix[0], node_couple[0],
    )
    return (
        solved,
        skel.reshape(columns, blocks, width),
        node_solution[None],
        node_skeleton[None],
    )


def solution(mesh):
    return jax.shard_map(
        on_device,
        mesh=mesh,
        in_specs=(
            P("cells", "rhs", None),
            P("cells", None, None),
            P("cells", None, None, None),
            P("cells", None),
            P("rhs", "cells", None),
            P("cells", None, "rhs"),
            P("cells", None, "rhs"),
            P("cells", None, "rhs"),
        ),
        out_specs=(
            P("cells", "rhs", None),
            P("rhs", "cells", None),
            P("cells", "rhs", None),
            P("cells", "rhs", None),
        ),
        check_vma=False,
    )
```

time: 174 us -> 104 us (0.60)
  Pallas kernels: 0 us -> 97 us
  waiting for transfers between devices: 62.1 us -> 0 us
  other arithmetic: 28.4 us -> 0.69 us
  starting transfers between devices: 27.1 us -> 0 us
  matrix products: 19.8 us -> 0 us
  between operations: 14.2 us -> 0.66 us
  blocking collectives: 8.3 us -> 0 us
  local copies, waits for them, and re-layouts: 12.8 us -> 5.57 us
    pallas_call x0 -> x2, Pallas kernels: none -> 97 us  [the longest x1 84.9 us: tree_call(): pl.pallas_call(functools.partial(tree_kernel, n, levels), out_shape=[jax....]
    ppermute x10 -> x0, waiting for transfers between devices: 61.4 us -> none  [the longest x4 39.5 us: passed_along(): lax.ppermute(value, axis, [(source, source + steps) for source in range(i...]
    ppermute x10 -> x0, starting transfers between devices: 27.1 us -> none  [the longest x4 13.7 us: passed_along(): lax.ppermute(value, axis, [(source, source + steps) for source in range(i...]
    dot_general x9 -> x0, matrix products: 19.8 us -> none  [the longest x7 11 us: multiply(): jnp.dot(operand, gathered[which_op], preferred_element_type=jnp.float32)]
    scatter-add x1 -> x0, other arithmetic: 16.6 us -> none  [on_device(): jax.ops.segment_sum(updates, segment_ids, num_segments=span_rows * blocks)]
    all_gather x1 -> x0, blocking collectives: 8.3 us -> none  [on_device(): lax.all_gather(node_couple[0], 'rhs', axis=1, tiled=True)]
    convert_element_type x1 -> x0, other arithmetic: 6.57 us -> none  [on_device(): skeleton_rhs.reshape(columns, blocks * block_width).astype(jnp.bfloat16)]
    broadcast_in_dim x1 -> x0, local copies, waits for them, and re-layouts: 5.61 us -> none  [on_device(): jax.ops.segment_sum(updates, segment_ids, num_segments=span_rows * blocks)]
  transfers between devices with their start and end apart: 12 -> 0, of which waited for: 8 -> 0; matrix products, arithmetic and copies ran while one was open for 31% -> 0% of each run, Pallas kernels for 0% -> 0%
where the time goes in v1:
time: 104 us
  Pallas kernels  97 us (93%)
  local copies, waits for them, and re-layouts  5.57 us (5%)
    pallas_call x1, Pallas kernels, tree_call(): pl.pallas_call(functools.partial(tree_kernel, n, levels), out_shape=[jax....  84.9 us
    pallas_call x1, Pallas kernels, leaf_call(): pl.pallas_call(functools.partial(leaf_kernel, blocks, slots), grid_spec=g...  12.1 us
    unnamed x13, local copies, waits for them, and re-layouts  5.49 us

profile of v1, /device:TPU:0, one launch (start us, length us, event | category | flops | bytes accessed | tf_op | source)
XLA Modules:
  0.0 103.9 jit_solution(1496158529553442016)
XLA Ops:
  0.6 0.7 broadcast_subtract_fusion
  1.3 0.1 sub.14.seg_ref
  1.4 0.0 copy-start
  1.4 1.7 %copy-done = bf16[8,384,384]{2,1,0:T(8,128)(2,1)S(1)} copy-done((bf16[8,384,384]{2,1,0:T(8,128)(2,1)S(1)}, bf16[8,384,384]{2,1,0:T(8,128)(2,1)}, u32[]{:S(2)}) %copy-start) | copy-done | bytes 2359320
  3.1 0.0 copy-start.2
  3.1 1.1 %copy-done.2 = bf16[8,128,384]{2,1,0:T(8,128)(2,1)S(1)} copy-done((bf16[8,128,384]{2,1,0:T(8,128)(2,1)S(1)}, bf16[8,128,384]{2,1,0:T(8,128)(2,1)}, u32[]{:S(2)}) %copy-start.2) | copy-done | bytes 786456
  4.2 0.0 copy-start.1
  4.2 0.0 copy-start.3
  4.2 0.0 copy-start.4
  4.2 12.1 %shard_map.111 = (bf16[8,128,384]{2,1,0:T(8,128)(2,1)}, f32[32,128,128]{2,1,0:T(8,128)S(1)}, bf16[4,32,128,128]{3,2,1,0:T(8,128)(2,1)}) custom-call(s32[72]{0:T(128)S(1)} %sub.14.seg_ref, bf16[8,128,384]{2,1,0:T(8,128)(2,1)S(1)} %copy-done.2, bf16[8,384,384]{2,1,0:T(8,128)(2,1)S(1)} %copy-done, bf16[8,9,384,128]{3,2,1,0:T(8,128)(2,1)} %couple_ref.1), custom_call_target="tpu_custom_call" | custom-call | tf_op jit(solution)/shard_map/pallas_call | solution.py:74
  16.3 0.0 copy-done.1
  16.3 0.0 copy-done.3
  16.3 0.0 copy-done.4
  16.3 84.9 %shard_map.112 = (f32[4096,128]{1,0:T(8,128)S(1)}, bf16[128,512]{1,0:T(8,128)(2,1)S(1)}, f32[128,512]{1,0:T(8,128)S(1)}) custom-call(bf16[4,32,128,128]{3,2,1,0:T(8,128)(2,1)} %get-tuple-element.11.send, f32[32,128,128]{2,1,0:T(8,128)S(1)} %get-tuple-element.12.own, f32[4096,128]{1,0:T(8,128)} %bitcast.13, bf16[4096,128]{1,0:T(8,128)(2,1)S(1)} %bitcast.8, ...), custom_call_target="tpu_custom_call" | custom-call | tf_op jit(solution)/shard_map/pallas_call | solution.py:289
  101.3 1.3 %copy.15 = f32[128,32,128]{2,1,0:T(8,128)} copy(f32[128,32,128]{2,1,0:T(8,128)S(1)} %bitcast.7) | data formatting | bytes 4194304
  102.6 0.7 copy.16
  103.2 0.7 copy.17
Async XLA Ops:
  1.4 1.7 %copy-start = (bf16[8,384,384]{2,1,0:T(8,128)(2,1)S(1)}, bf16[8,384,384]{2,1,0:T(8,128)(2,1)}, u32[]{:S(2)}) copy-start(bf16[8,384,384]{2,1,0:T(8,128)(2,1)} %inv_ref.1) | copy-start | bytes 7077892
  3.1 1.1 %copy-start.2 = (bf16[8,128,384]{2,1,0:T(8,128)(2,1)S(1)}, bf16[8,128,384]{2,1,0:T(8,128)(2,1)}, u32[]{:S(2)}) copy-start(bf16[8,128,384]{2,1,0:T(8,128)(2,1)} %x_ref.1) | copy-start | bytes 2359300
  4.2 12.1 %copy-start.1 = (bf16[1,4096,128]{2,1,0:T(8,128)(2,1)S(1)}, bf16[1,4096,128]{2,1,0:T(8,128)(2,1)}, u32[]{:S(2)}) copy-start(bf16[1,4096,128]{2,1,0:T(8,128)(2,1)} %param.13) | copy-start | bytes 3145732
  4.2 12.1 %copy-start.3 = (bf16[1,1024,128]{2,1,0:T(8,128)(2,1)S(1)}, bf16[1,1024,128]{2,1,0:T(8,128)(2,1)}, u32[]{:S(2)}) copy-start(bf16[1,1024,128]{2,1,0:T(8,128)(2,1)} %param.14) | copy-start | bytes 786436
  4.2 12.1 %copy-start.4 = (bf16[1,512,128]{2,1,0:T(8,128)(2,1)S(1)}, bf16[1,512,128]{2,1,0:T(8,128)(2,1)}, u32[]{:S(2)}) copy-start(bf16[1,512,128]{2,1,0:T(8,128)(2,1)} %param.15) | copy-start | bytes 393220

commit v2 on v1

--- a/solution.py
+++ b/solution.py
@@ -8,7 +8,6 @@
 from jax.sharding import PartitionSpec as P
 
 HOP = 2
-DISTANCES = (-2, -1, 1, 2)
 CHUNKS = 4
 MESH = pl.DeviceIdType.MESH
 F32, BF16 = jnp.float32, jnp.bfloat16
@@ -79,15 +78,16 @@
             jax.ShapeDtypeStruct((blocks, columns, width), F32),
             jax.ShapeDtypeStruct((2 * HOP, blocks, columns, width), BF16),
         ],
-        compiler_params=pltpu.CompilerParams(vmem_limit_bytes=48 * 2**20),
+        compiler_params=pltpu.CompilerParams(vmem_limit_bytes=60 * 2**20),
     )(segments, right_side, leaf_inverse, leaf_couple)
 
 
 def tree_kernel(
     n, levels, send, own, skel, lift, mix, couple, out_skel, out_sol, out_node,
-    recv, own_v, skel_v, flat, lift_g, mix_g, couple_g, mine, left_v, right_v, sol_v,
+    recv, relay, addend, own_v, skel_v, flat, lift_g, mix_g, couple_g, mix_h, couple_h,
+    mine, left_v, right_v,
     local_sem, port_send, port_recv, near_send, near_recv, far_send, far_recv, fwd_send, fwd_recv,
-    vec_send, vec_recv,
+    half_send, half_recv, vec_send, vec_recv,
 ):
     me = lax.axis_index("cells")
     rank = lax.axis_index("rhs")
@@ -98,6 +98,14 @@
     node = couple_g.shape[0]
     reach = [max(1, 2 ** (level - 2)) for level in range(1, levels + 1)]
     partners = sorted({s % n for d in reach + [1, 2, n // 2] for s in (d, -d)})
+    odd = me % 2
+    side = 2 * odd - 1
+    diag_slot, beside_slot, ahead_slot, behind_slot = 1 + odd, 2 - odd, 3 * odd, 3 - 3 * odd
+    beside = me - side
+    ahead, behind = me + 2 * side, me - 2 * side
+    has_ahead = jnp.logical_and(ahead >= 0, ahead < n)
+    has_behind = jnp.logical_and(behind >= 0, behind < n)
+    ahead, behind = (ahead + n) % n, (behind + n) % n
 
     barrier = pltpu.get_barrier_semaphore()
     for step in partners:
@@ -118,98 +126,169 @@
     group = blocks // CHUNKS
     depth = lift.shape[0] // CHUNKS
     pieces = [(lift, lift_g, pl.ds(q * depth, depth)) for q in range(CHUNKS)]
-    pieces += [(mix, mix_g, pl.ds(0, mix.shape[0])), (couple, couple_g, pl.ds(0, couple.shape[0]))]
+    pieces += [(mix, mix_g, pl.ds(0, mix.shape[0])), (couple, couple_g, pl.ds(0, node))]
+    count = len(pieces)
+    halves = [(mix, mix_h, pl.ds(0, node)), (mix, mix_h, pl.ds(node, node)), (couple, couple_h, pl.ds(0, node))]
+
+    def place(i, which):
+        _, dst, rows = (pieces + halves)[i]
+        return dst.at[rows, shard(which)]
+
+    def source(i):
+        return pieces[i][0].at[pieces[i][2]] if i < count else place(i, rank)
 
     def to_near(i):
-        src, dst, rows = pieces[i]
-        return remote(src.at[rows], dst.at[rows, shard(rank)], near_send.at[i], near_recv.at[i], me, near)
+        return remote(source(i), place(i, rank), near_send.at[i], near_recv.at[i], me, near)
 
     def to_far(i):
-        src, dst, rows = pieces[i]
-        return remote(src.at[rows], dst.at[rows, shard(rank)], far_send.at[i], far_recv.at[i], me, far)
+        return remote(source(i), place(i, rank), far_send.at[i], far_recv.at[i], me, far)
 
     def forward(i):
-        _, dst, rows = pieces[i]
-        place = dst.at[rows, shard(far)]
-        return remote(place, place, fwd_send.at[i], fwd_recv.at[i], me, near)
+        return remote(place(i, far), place(i, far), fwd_send.at[i], fwd_recv.at[i], me, near)
 
     def near_arrival(i):
-        _, dst, rows = pieces[i]
-        place = dst.at[rows, shard(near)]
-        return remote(place, place, near_send.at[i], near_recv.at[i], me, near)
+        return remote(place(i, near), place(i, near), near_send.at[i], near_recv.at[i], me, near)
 
     def far_arrival(i):
-        _, dst, rows = pieces[i]
-        place = dst.at[rows, shard(far)]
-        return remote(place, place, far_send.at[i], far_recv.at[i], me, far)
+        return remote(place(i, far), place(i, far), far_send.at[i], far_recv.at[i], me, far)
 
     def fwd_arrival(i):
-        _, dst, rows = pieces[i]
-        place = dst.at[rows, shard(far_near)]
-        return remote(place, place, fwd_send.at[i], fwd_recv.at[i], me, near)
-
-    def portion(j, q):
-        rows = pl.ds(q * group, group)
+        return remote(place(i, far_near), place(i, far_near), fwd_send.at[i], fwd_recv.at[i], me, near)
+
+    def across(i):
+        src, dst, rows = halves[i]
         return remote(
-            send.at[j, rows], recv.at[j, rows], port_send.at[j, q], port_recv.at[j, q],
-            (me + DISTANCES[j] + n) % n, rank,
+            src.at[rows], dst.at[rows, shard(rank)], half_send.at[i], half_recv.at[i],
+            (me + n // 2) % n, rank,
         )
 
-    def sends_to(j):
-        target = me + DISTANCES[j]
-        return jnp.logical_and(target >= 0, target < n)
-
-    def hears_from(j):
-        source = me - DISTANCES[j]
-        return jnp.logical_and(source >= 0, source < n)
-
-    to_far(0).start()
-    for q in range(CHUNKS):
-        for j in range(len(DISTANCES)):
-            @pl.when(sends_to(j))
-            def _():
-                portion(j, q).start()
-        if q == 0:
-            for i in range(1, len(pieces)):
-                to_far(i).start()
-    for i in range(len(pieces)):
+    first_half = CHUNKS // 2
+
+    def rows_of(q):
+        return pl.ds(q * group, group)
+
+    def rows_in_half(q):
+        return pl.ds((q % first_half) * group, group)
+
+    def diag(q):
+        at = 0 if q < first_half else 1
+        return remote(
+            send.at[diag_slot, rows_of(q)], relay.at[at, rows_in_half(q)],
+            port_send.at[0, q], port_recv.at[0, q], beside if at == 0 else ahead, rank,
+        )
+
+    def to_beside(q):
+        src = send.at[beside_slot, rows_of(q)] if q < first_half else addend.at[1, rows_in_half(q)]
+        return remote(src, recv.at[0, rows_of(q)], port_send.at[1, q], port_recv.at[1, q], beside, rank)
+
+    def to_ahead(q):
+        return remote(
+            send.at[ahead_slot, rows_of(q)], recv.at[1, rows_of(q)],
+            port_send.at[2, q], port_recv.at[2, q], ahead, rank,
+        )
+
+    def to_behind(q):
+        src = send.at[behind_slot, rows_of(q)] if q >= first_half else addend.at[0, rows_in_half(q)]
+        return remote(src, recv.at[2, rows_of(q)], port_send.at[3, q], port_recv.at[3, q], behind, rank)
+
+    addends = [
+        pltpu.make_async_copy(send.at[behind_slot, pl.ds(0, blocks // 2)], addend.at[0], local_sem.at[0]),
+        pltpu.make_async_copy(send.at[beside_slot, pl.ds(blocks // 2, blocks // 2)], addend.at[1], local_sem.at[1]),
+    ]
+    for at in range(first_half):
+        @pl.when(has_ahead)
+        def _():
+            diag(at).start()
+            diag(at + first_half).start()
+
+        @pl.when(has_behind)
+        def _():
+            to_behind(at + first_half).start()
+
+        to_far(at).start()
+    for copy in addends:
+        copy.start()
+    for at in range(first_half):
+        to_beside(at).start()
+
+        @pl.when(has_ahead)
+        def _():
+            to_ahead(at).start()
+
+        to_far(at + first_half).start()
+    for i in range(CHUNKS, count):
+        to_far(i).start()
+
+    @pl.when(has_ahead)
+    def _():
+        for q in range(first_half, CHUNKS):
+            to_ahead(q).start()
+
+    for i in range(count):
         to_near(i).start()
     locals_ = [
-        pltpu.make_async_copy(own, own_v, local_sem.at[0]),
-        pltpu.make_async_copy(skel, skel_v, local_sem.at[1]),
+        pltpu.make_async_copy(own, own_v, local_sem.at[2]),
+        pltpu.make_async_copy(skel, skel_v, local_sem.at[3]),
     ]
     for i, (src, dst, rows) in enumerate(pieces):
-        locals_.append(pltpu.make_async_copy(src.at[rows], dst.at[rows, shard(rank)], local_sem.at[2 + i]))
+        locals_.append(pltpu.make_async_copy(src.at[rows], dst.at[rows, shard(rank)], local_sem.at[4 + i]))
     for copy in locals_:
         copy.start()
 
-    for j in range(len(DISTANCES)):
-        @pl.when(jnp.logical_not(hears_from(j)))
+    for slot, there in ((1, has_behind), (2, has_ahead)):
+        @pl.when(jnp.logical_not(there))
         def _():
             @pl.loop(0, blocks)
             def _(b):
-                recv[j, b] = jnp.zeros((columns, width), BF16)
+                recv[slot, b] = jnp.zeros((columns, width), BF16)
 
     for copy in locals_:
         copy.wait()
+    for b in range(blocks):
+        own_v[b] = skel_v[pl.ds(b, columns, stride=blocks), :] - own_v[b]
+    for copy in addends:
+        copy.wait()
+
+    for at in range(2):
+        for q in range(at * first_half, (at + 1) * first_half):
+            @pl.when(has_behind)
+            def _():
+                diag(q).wait_recv()
+
+                @pl.loop((q % first_half) * group, (q % first_half + 1) * group)
+                def _(b):
+                    addend[at, b] = (addend[at, b].astype(F32) + relay[at, b].astype(F32)).astype(BF16)
+
+                if at == 0:
+                    to_behind(q).start()
+
+            if at == 1:
+                to_beside(q).start()
+        far_arrival(at).wait_recv()
+        forward(at).start()
 
     total = None
     for q in range(CHUNKS):
-        ready = [q] if q < CHUNKS - 1 else list(range(q, len(pieces)))
-        for i in ready:
+        for i in ([], [2], [3], list(range(CHUNKS, count)))[q]:
             far_arrival(i).wait_recv()
             forward(i).start()
-        for j in range(len(DISTANCES)):
-            @pl.when(hears_from(j))
-            def _():
-                portion(j, q).wait_recv()
+        to_beside(q).wait_recv()
+
+        @pl.when(has_behind)
+        def _():
+            to_ahead(q).wait_recv()
+
+        @pl.when(has_ahead)
+        def _():
+            to_behind(q).wait_recv()
+
+        if q == CHUNKS - 1:
+            for i in range(len(halves)):
+                across(i).start()
         for b in range(q * group, (q + 1) * group):
-            rows = pl.ds(b, columns, stride=blocks)
-            arrived = own_v[b]
-            for j in range(len(DISTANCES)):
-                arrived = arrived + recv[j, b].astype(F32)
-            value = skel_v[rows, :] - arrived
-            skel_v[rows, :] = value
+            arrived = recv[0, b].astype(F32) + recv[1, b].astype(F32) + recv[2, b].astype(F32)
+            value = own_v[b] - arrived
+            skel_v[pl.ds(b, columns, stride=blocks), :] = value
             flat[:, b * width : (b + 1) * width] = value.astype(BF16)
         near_arrival(q).wait_recv()
         fwd_arrival(q).wait_recv()
@@ -223,13 +302,17 @@
     result = pltpu.make_async_copy(skel_v, out_skel, local_sem.at[0])
     sent = []
 
-    def merge(first, second):
-        solved = (dot(first, mix_g[:node, :]) + dot(second, mix_g[node:, :])).astype(BF16)
-        skeleton = 0.5 * (first.astype(F32) + second.astype(F32)) - dot(solved, couple_g[...])
+    def merge(first, second, mixing, coupling):
+        solved = (dot(first, mixing[:node, :]) + dot(second, mixing[node:, :])).astype(BF16)
+        skeleton = 0.5 * (first.astype(F32) + second.astype(F32)) - dot(solved, coupling[...])
         return solved, skeleton
 
-    solved = None
-    for level in range(levels):
+    def pass_on(i):
+        across(i).wait_recv()
+        to_far(count + i).start()
+        to_near(count + i).start()
+
+    for level in range(levels - 1):
         d = reach[level]
         up = vector(mine.at[level], left_v.at[level], 2 * level, d)
         up.start()
@@ -240,7 +323,7 @@
             sent.append(down)
         else:
             result.start()
-            for i in range(CHUNKS, len(pieces)):
+            for i in range(CHUNKS, count):
                 near_arrival(i).wait_recv()
                 fwd_arrival(i).wait_recv()
         up.wait_recv()
@@ -249,32 +332,50 @@
             second = right_v[level]
         else:
             second = mine[0]
-        solved, skeleton = merge(left_v[level], second)
-        if level == levels - 1:
-            sol_v[...] = solved
-            other = vector(sol_v, right_v.at[0], 2 * levels, n // 2)
-            other.start()
+        _, skeleton = merge(left_v[level], second, mix_g, couple_g)
         mine[level + 1] = skeleton.astype(BF16)
-    up = vector(mine.at[levels], left_v.at[levels], 2 * levels + 1, n // 2)
+
+    last = levels - 1
+    up = vector(mine.at[last], left_v.at[last], 2 * last, reach[last])
+    down = vector(mine.at[last], right_v.at[last], 2 * last + 1, -reach[last])
     up.start()
-    sent += [other, up]
-    other.wait_recv()
+    down.start()
+    sent += [up, down]
+    for i in range(len(halves)):
+        pass_on(i)
+    for i in range(count, count + len(halves)):
+        far_arrival(i).wait_recv()
+        forward(i).start()
     up.wait_recv()
-    solved, skeleton = merge(left_v[levels], right_v[0])
+    down.wait_recv()
+    for i in range(count, count + len(halves)):
+        near_arrival(i).wait_recv()
+        fwd_arrival(i).wait_recv()
+    solved, skeleton = merge(right_v[last], left_v[last], mix_h, couple_h)
+    solved, skeleton = merge(skeleton.astype(BF16), solved, mix_g, couple_g)
     out_sol[...] = solved
     out_node[...] = skeleton
 
     for copy in sent:
         copy.wait_send()
-    for i in range(len(pieces)):
+    for i in range(count + len(halves)):
         to_near(i).wait_send()
         to_far(i).wait_send()
         forward(i).wait_send()
-    for j in range(len(DISTANCES)):
-        @pl.when(sends_to(j))
-        def _():
-            for q in range(CHUNKS):
-                portion(j, q).wait_send()
+    for i in range(len(halves)):
+        across(i).wait_send()
+    for q in range(CHUNKS):
+        to_beside(q).wait_send()
+
+        @pl.when(has_ahead)
+        def _():
+            diag(q).wait_send()
+            to_ahead(q).wait_send()
+
+        @pl.when(has_behind)
+        def _():
+            to_behind(q).wait_send()
+
     result.wait()
 
 
@@ -282,7 +383,7 @@
     blocks, columns, width = own.shape
     node = couple.shape[0]
     levels = n.bit_length() - 1
-    pieces = CHUNKS + 2
+    pieces = CHUNKS + 2 + 3
     dma = pltpu.SemaphoreType.DMA
     vmem = pl.BlockSpec(memory_space=pltpu.VMEM)
     hbm = pl.BlockSpec(memory_space=pl.ANY)
@@ -296,27 +397,31 @@
         in_specs=[hbm] * 6,
         out_specs=[hbm, vmem, vmem],
         scratch_shapes=[
-            pltpu.VMEM((2 * HOP, blocks, columns, width), BF16),
+            pltpu.VMEM((3, blocks, columns, width), BF16),
+            pltpu.VMEM((2, blocks // 2, columns, width), BF16),
+            pltpu.VMEM((2, blocks // 2, columns, width), BF16),
             pltpu.VMEM((blocks, columns, width), F32),
             pltpu.VMEM(skel.shape, F32),
             pltpu.VMEM((columns, blocks * width), BF16),
             pltpu.VMEM((lift.shape[0], node), BF16),
             pltpu.VMEM((mix.shape[0], node), BF16),
             pltpu.VMEM((couple.shape[0], node), BF16),
-            pltpu.VMEM((levels + 1, columns, node), BF16),
-            pltpu.VMEM((levels + 1, columns, node), BF16),
+            pltpu.VMEM((mix.shape[0], node), BF16),
+            pltpu.VMEM((couple.shape[0], node), BF16),
             pltpu.VMEM((levels, columns, node), BF16),
-            pltpu.VMEM((columns, node), BF16),
-            dma((2 + pieces,)),
-            dma((2 * HOP, CHUNKS)),
-            dma((2 * HOP, CHUNKS)),
+            pltpu.VMEM((levels, columns, node), BF16),
+            pltpu.VMEM((levels, columns, node), BF16),
+            dma((4 + CHUNKS + 2,)),
+            dma((4, CHUNKS)),
+            dma((4, CHUNKS)),
             dma((pieces,)), dma((pieces,)), dma((pieces,)),
             dma((pieces,)), dma((pieces,)), dma((pieces,)),
-            dma((2 * levels + 2,)),
-            dma((2 * levels + 2,)),
+            dma((3,)), dma((3,)),
+            dma((2 * levels,)),
+            dma((2 * levels,)),
         ],
         compiler_params=pltpu.CompilerParams(
-            collective_id=0, has_side_effects=True, vmem_limit_bytes=48 * 2**20
+            collective_id=0, has_side_effects=True, vmem_limit_bytes=60 * 2**20
         ),
     )(send, own, skel, lift, mix, couple)
 

time: 104 us -> 99 us (0.952)
  the two profiles are of different devices: /device:TPU:0 before, /device:TPU:11 now
where the time goes in v2:
time: 99 us; the launch traced here: 98.6 us
  Pallas kernels  92.2 us (93%)
  local copies, waits for them, and re-layouts  5.09 us (5%)
    pallas_call x1, Pallas kernels, tree_call(): pl.pallas_call(functools.partial(tree_kernel, n, levels), out_shape=[jax....  78.7 us
    pallas_call x1, Pallas kernels, leaf_call(): pl.pallas_call(functools.partial(leaf_kernel, blocks, slots), grid_spec=g...  13.5 us
    unnamed x7, local copies, waits for them, and re-layouts  4.5 us

profile of v2, /device:TPU:11, one launch (start us, length us, event | category | flops | bytes accessed | tf_op | source)
XLA Modules:
  0.0 98.6 jit_solution(14013121707344404275)
XLA Ops:
  0.6 0.7 broadcast_subtract_fusion
  1.3 0.6 sub.14.seg_ref
  1.9 13.5 %shard_map.111 = (bf16[8,128,384]{2,1,0:T(8,128)(2,1)}, f32[32,128,128]{2,1,0:T(8,128)}, bf16[4,32,128,128]{3,2,1,0:T(8,128)(2,1)}) custom-call(s32[72]{0:T(128)} %sub.14.seg_ref, bf16[8,128,384]{2,1,0:T(8,128)(2,1)} %x_ref.1, bf16[8,384,384]{2,1,0:T(8,128)(2,1)} %inv_ref.1, bf16[8,9,384,128]{3,2,1,0:T(8,128)(2,1)} %couple_ref.1), custom_call_target="tpu_custom_call" | custom-call | tf_op jit(solution)/shard_map/pallas_call | solution.py:73
  15.4 78.7 %shard_map.112 = (f32[4096,128]{1,0:T(8,128)}, bf16[128,512]{1,0:T(8,128)(2,1)}, f32[128,512]{1,0:T(8,128)}) custom-call(bf16[4,32,128,128]{3,2,1,0:T(8,128)(2,1)} %get-tuple-element.11.send, f32[32,128,128]{2,1,0:T(8,128)} %get-tuple-element.12.own, f32[4096,128]{1,0:T(8,128)} %bitcast.7, bf16[4096,128]{1,0:T(8,128)(2,1)} %bitcast.9, ...), custom_call_target="tpu_custom_call" | custom-call | tf_op jit(solution)/shard_map/pallas_call | solution.py:390
  94.1 0.0 copy-start.1
  94.1 0.0 copy-start
  94.1 3.1 %copy.15 = f32[128,32,128]{2,1,0:T(8,128)} copy(f32[128,32,128]{2,1,0:T(8,128)} %bitcast.8) | data formatting | bytes 4194304
  97.3 0.0 copy-done.1
  97.3 0.7 copy.16
  97.9 0.0 copy-done
  97.9 0.7 copy.17
Async XLA Ops:
  94.1 3.2 %copy-start.1 = (bf16[128,512]{1,0:T(8,128)(2,1)S(1)}, bf16[128,512]{1,0:T(8,128)(2,1)}, u32[]{:S(2)}) copy-start(bf16[128,512]{1,0:T(8,128)(2,1)} %get-tuple-element.14) | copy-start | bytes 393220
  94.1 3.8 %copy-start = (f32[128,512]{1,0:T(8,128)S(1)}, f32[128,512]{1,0:T(8,128)}, u32[]{:S(2)}) copy-start(f32[128,512]{1,0:T(8,128)} %get-tuple-element.15) | copy-start | bytes 786436

commit v3 on v2

--- a/solution.py
+++ b/solution.py
@@ -17,76 +17,12 @@
     return jnp.dot(a, b, preferred_element_type=F32)
 
 
-def leaf_kernel(blocks, slots, seg_ref, x_ref, inv_ref, couple_ref, sol_ref, own_ref, send_ref, acc):
-    cell = pl.program_id(0)
-
-    @pl.when(cell == 0)
-    def _():
-        @pl.loop(0, acc.shape[0])
-        def _(i):
-            acc[i] = jnp.zeros(acc.shape[1:], F32)
-
-    solved = dot(x_ref[0], inv_ref[0]).astype(BF16)
-    sol_ref[0] = solved
-    width = couple_ref.shape[-1]
-    for k in range(0, slots, 2):
-        pair = [j for j in (k, k + 1) if j < slots]
-        wide = jnp.concatenate([couple_ref[0, j] for j in pair], axis=1)
-        update = dot(solved, wide)
-        for at, j in enumerate(pair):
-            where = seg_ref[cell * slots + j]
-            acc[where] += update[:, at * width : (at + 1) * width]
-
-    @pl.when(cell == pl.num_programs(0) - 1)
-    def _():
-        for row in range(2 * HOP + 1):
-            if row == HOP:
-                @pl.loop(0, blocks)
-                def _(b):
-                    own_ref[b] = acc[row * blocks + b]
-            else:
-                slot = row if row < HOP else row - 1
-
-                @pl.loop(0, blocks)
-                def _(b):
-                    send_ref[slot, b] = acc[row * blocks + b].astype(BF16)
-
-
-def leaf_call(segments, right_side, leaf_inverse, leaf_couple, blocks):
-    cells, columns, rw = right_side.shape
-    slots, width = leaf_couple.shape[1], leaf_couple.shape[3]
-    grid_spec = pltpu.PrefetchScalarGridSpec(
-        num_scalar_prefetch=1,
-        grid=(cells,),
-        in_specs=[
-            pl.BlockSpec((1, columns, rw), lambda c, s: (c, 0, 0)),
-            pl.BlockSpec((1, rw, rw), lambda c, s: (c, 0, 0)),
-            pl.BlockSpec((1, slots, rw, width), lambda c, s: (c, 0, 0, 0)),
-        ],
-        out_specs=[
-            pl.BlockSpec((1, columns, rw), lambda c, s: (c, 0, 0)),
-            pl.BlockSpec((blocks, columns, width), lambda c, s: (0, 0, 0)),
-            pl.BlockSpec((2 * HOP, blocks, columns, width), lambda c, s: (0, 0, 0, 0)),
-        ],
-        scratch_shapes=[pltpu.VMEM(((2 * HOP + 1) * blocks, columns, width), F32)],
-    )
-    return pl.pallas_call(
-        functools.partial(leaf_kernel, blocks, slots),
-        grid_spec=grid_spec,
-        out_shape=[
-            jax.ShapeDtypeStruct((cells, columns, rw), BF16),
-            jax.ShapeDtypeStruct((blocks, columns, width), F32),
-            jax.ShapeDtypeStruct((2 * HOP, blocks, columns, width), BF16),
-        ],
-        compiler_params=pltpu.CompilerParams(vmem_limit_bytes=60 * 2**20),
-    )(segments, right_side, leaf_inverse, leaf_couple)
-
-
 def tree_kernel(
-    n, levels, send, own, skel, lift, mix, couple, out_skel, out_sol, out_node,
-    recv, relay, addend, own_v, skel_v, flat, lift_g, mix_g, couple_g, mix_h, couple_h,
+    n, levels, prev, last_of, rhs, inverse, leaf_couple, skel, lift, mix, couple,
+    out_leaf, out_skel, out_sol, out_node,
+    rhs_v, inverse_v, leaf_couple_v, leaf_v, partial, send, recv, relay, own_v, skel_v, flat, lift_g, mix_g, couple_g, mix_h, couple_h,
     mine, left_v, right_v,
-    local_sem, port_send, port_recv, near_send, near_recv, far_send, far_recv, fwd_send, fwd_recv,
+    leaf_sem, local_sem, port_send, port_recv, near_send, near_recv, far_send, far_recv, fwd_send, fwd_recv,
     half_send, half_recv, vec_send, vec_recv,
 ):
     me = lax.axis_index("cells")
@@ -100,12 +36,27 @@
     partners = sorted({s % n for d in reach + [1, 2, n // 2] for s in (d, -d)})
     odd = me % 2
     side = 2 * odd - 1
-    diag_slot, beside_slot, ahead_slot, behind_slot = 1 + odd, 2 - odd, 3 * odd, 3 - 3 * odd
     beside = me - side
     ahead, behind = me + 2 * side, me - 2 * side
     has_ahead = jnp.logical_and(ahead >= 0, ahead < n)
     has_behind = jnp.logical_and(behind >= 0, behind < n)
     ahead, behind = (ahead + n) % n, (behind + n) % n
+
+    DIAG, BESIDE, AHEAD, BEHIND = range(4)
+    row_of = (HOP + side, HOP - side, HOP + 2 * side, HOP - 2 * side)
+
+    cells, slots = leaf_couple.shape[0], leaf_couple.shape[1]
+
+    def leaf_copies(c):
+        return [
+            pltpu.make_async_copy(rhs.at[c], rhs_v.at[c], leaf_sem.at[0, c]),
+            pltpu.make_async_copy(inverse.at[c], inverse_v.at[c], leaf_sem.at[1, c]),
+            pltpu.make_async_copy(leaf_couple.at[c], leaf_couple_v.at[c], leaf_sem.at[2, c]),
+        ]
+
+    for c in range(cells):
+        for copy in leaf_copies(c):
+            copy.start()
 
     barrier = pltpu.get_barrier_semaphore()
     for step in partners:
@@ -173,67 +124,85 @@
     def diag(q):
         at = 0 if q < first_half else 1
         return remote(
-            send.at[diag_slot, rows_of(q)], relay.at[at, rows_in_half(q)],
+            send.at[DIAG, rows_of(q)], relay.at[at, rows_in_half(q)],
             port_send.at[0, q], port_recv.at[0, q], beside if at == 0 else ahead, rank,
         )
 
     def to_beside(q):
-        src = send.at[beside_slot, rows_of(q)] if q < first_half else addend.at[1, rows_in_half(q)]
-        return remote(src, recv.at[0, rows_of(q)], port_send.at[1, q], port_recv.at[1, q], beside, rank)
+        return remote(send.at[BESIDE, rows_of(q)], recv.at[0, rows_of(q)], port_send.at[1, q], port_recv.at[1, q], beside, rank)
 
     def to_ahead(q):
         return remote(
-            send.at[ahead_slot, rows_of(q)], recv.at[1, rows_of(q)],
+            send.at[AHEAD, rows_of(q)], recv.at[1, rows_of(q)],
             port_send.at[2, q], port_recv.at[2, q], ahead, rank,
         )
 
     def to_behind(q):
-        src = send.at[behind_slot, rows_of(q)] if q >= first_half else addend.at[0, rows_in_half(q)]
-        return remote(src, recv.at[2, rows_of(q)], port_send.at[3, q], port_recv.at[3, q], behind, rank)
-
-    addends = [
-        pltpu.make_async_copy(send.at[behind_slot, pl.ds(0, blocks // 2)], addend.at[0], local_sem.at[0]),
-        pltpu.make_async_copy(send.at[beside_slot, pl.ds(blocks // 2, blocks // 2)], addend.at[1], local_sem.at[1]),
-    ]
-    for at in range(first_half):
-        @pl.when(has_ahead)
-        def _():
-            diag(at).start()
-            diag(at + first_half).start()
-
-        @pl.when(has_behind)
-        def _():
-            to_behind(at + first_half).start()
-
-        to_far(at).start()
-    for copy in addends:
-        copy.start()
-    for at in range(first_half):
-        to_beside(at).start()
-
-        @pl.when(has_ahead)
-        def _():
-            to_ahead(at).start()
-
-        to_far(at + first_half).start()
-    for i in range(CHUNKS, count):
+        return remote(send.at[BEHIND, rows_of(q)], recv.at[2, rows_of(q)], port_send.at[3, q], port_recv.at[3, q], behind, rank)
+
+    for i in range(2):
+        across(i).start()
+    for i in range(count):
         to_far(i).start()
-
-    @pl.when(has_ahead)
-    def _():
-        for q in range(first_half, CHUNKS):
-            to_ahead(q).start()
-
     for i in range(count):
         to_near(i).start()
-    locals_ = [
-        pltpu.make_async_copy(own, own_v, local_sem.at[2]),
-        pltpu.make_async_copy(skel, skel_v, local_sem.at[3]),
-    ]
+    locals_ = [pltpu.make_async_copy(skel, skel_v, local_sem.at[0])]
     for i, (src, dst, rows) in enumerate(pieces):
-        locals_.append(pltpu.make_async_copy(src.at[rows], dst.at[rows, shard(rank)], local_sem.at[4 + i]))
+        locals_.append(pltpu.make_async_copy(src.at[rows], dst.at[rows, shard(rank)], local_sem.at[1 + i]))
     for copy in locals_:
         copy.start()
+
+    @pl.loop(0, partial.shape[0])
+    def _(i):
+        partial[i] = jnp.zeros((columns, width), F32)
+
+    @pl.loop(0, cells)
+    def _(c):
+        for copy in leaf_copies(c):
+            copy.wait()
+        solved = dot(rhs_v[c], inverse_v[c]).astype(BF16)
+        leaf_v[c] = solved
+        for k in range(0, slots, 2):
+            pair = [j for j in (k, k + 1) if j < slots]
+            update = dot(solved, jnp.concatenate([leaf_couple_v[c, j] for j in pair], axis=1))
+            for at, j in enumerate(pair):
+                i = c * slots + j
+                partial[i] = update[:, at * width : (at + 1) * width] + partial[prev[i]]
+
+    def emit(role, q):
+        @pl.loop(q * group, (q + 1) * group)
+        def _(b):
+            send[role, b] = partial[last_of[row_of[role] * blocks + b]].astype(BF16)
+
+    for at in range(first_half):
+        for q in (at, at + first_half):
+            emit(DIAG, q)
+
+            @pl.when(has_ahead)
+            def _():
+                diag(q).start()
+
+        emit(BEHIND, at + first_half)
+
+        @pl.when(has_behind)
+        def _():
+            to_behind(at + first_half).start()
+
+    for q in range(CHUNKS):
+        if q < first_half:
+            emit(BESIDE, q)
+            to_beside(q).start()
+        emit(AHEAD, q)
+
+        @pl.when(has_ahead)
+        def _():
+            to_ahead(q).start()
+
+    leaf_out = pltpu.make_async_copy(leaf_v, out_leaf, leaf_sem.at[0, 0])
+    leaf_out.start()
+    for q in range(first_half):
+        emit(BEHIND, q)
+        emit(BESIDE, q + first_half)
 
     for slot, there in ((1, has_behind), (2, has_ahead)):
         @pl.when(jnp.logical_not(there))
@@ -245,19 +214,19 @@
     for copy in locals_:
         copy.wait()
     for b in range(blocks):
-        own_v[b] = skel_v[pl.ds(b, columns, stride=blocks), :] - own_v[b]
-    for copy in addends:
-        copy.wait()
+        own_v[b] = skel_v[pl.ds(b, columns, stride=blocks), :] - partial[last_of[HOP * blocks + b]]
 
     for at in range(2):
+        role = (BEHIND, BESIDE)[at]
         for q in range(at * first_half, (at + 1) * first_half):
             @pl.when(has_behind)
             def _():
                 diag(q).wait_recv()
 
-                @pl.loop((q % first_half) * group, (q % first_half + 1) * group)
+                @pl.loop(q * group, (q + 1) * group)
                 def _(b):
-                    addend[at, b] = (addend[at, b].astype(F32) + relay[at, b].astype(F32)).astype(BF16)
+                    passing = relay[at, b - at * (blocks // 2)].astype(F32)
+                    send[role, b] = (send[role, b].astype(F32) + passing).astype(BF16)
 
                 if at == 0:
                     to_behind(q).start()
@@ -266,12 +235,20 @@
                 to_beside(q).start()
         far_arrival(at).wait_recv()
         forward(at).start()
+
+    def pass_on(i):
+        across(i).wait_recv()
+        to_far(count + i).start()
+        to_near(count + i).start()
 
     total = None
     for q in range(CHUNKS):
         for i in ([], [2], [3], list(range(CHUNKS, count)))[q]:
             far_arrival(i).wait_recv()
             forward(i).start()
+        if q == 1:
+            for i in range(2):
+                pass_on(i)
         to_beside(q).wait_recv()
 
         @pl.when(has_behind)
@@ -283,8 +260,7 @@
             to_behind(q).wait_recv()
 
         if q == CHUNKS - 1:
-            for i in range(len(halves)):
-                across(i).start()
+            across(2).start()
         for b in range(q * group, (q + 1) * group):
             arrived = recv[0, b].astype(F32) + recv[1, b].astype(F32) + recv[2, b].astype(F32)
             value = own_v[b] - arrived
@@ -306,11 +282,6 @@
         solved = (dot(first, mixing[:node, :]) + dot(second, mixing[node:, :])).astype(BF16)
         skeleton = 0.5 * (first.astype(F32) + second.astype(F32)) - dot(solved, coupling[...])
         return solved, skeleton
-
-    def pass_on(i):
-        across(i).wait_recv()
-        to_far(count + i).start()
-        to_near(count + i).start()
 
     for level in range(levels - 1):
         d = reach[level]
@@ -326,6 +297,9 @@
             for i in range(CHUNKS, count):
                 near_arrival(i).wait_recv()
                 fwd_arrival(i).wait_recv()
+            for i in range(count, count + 2):
+                far_arrival(i).wait_recv()
+                forward(i).start()
         up.wait_recv()
         if level > 0:
             down.wait_recv()
@@ -341,11 +315,9 @@
     up.start()
     down.start()
     sent += [up, down]
-    for i in range(len(halves)):
-        pass_on(i)
-    for i in range(count, count + len(halves)):
-        far_arrival(i).wait_recv()
-        forward(i).start()
+    pass_on(2)
+    far_arrival(count + 2).wait_recv()
+    forward(count + 2).start()
     up.wait_recv()
     down.wait_recv()
     for i in range(count, count + len(halves)):
@@ -377,10 +349,12 @@
             to_behind(q).wait_send()
 
     result.wait()
-
-
-def tree_call(n, send, own, skel, lift, mix, couple):
-    blocks, columns, width = own.shape
+    leaf_out.wait()
+
+
+def tree_call(n, blocks, prev, last_of, rhs, inverse, leaf_couple, skel, lift, mix, couple):
+    cells, columns, _ = rhs.shape
+    slots, width = leaf_couple.shape[1], leaf_couple.shape[3]
     node = couple.shape[0]
     levels = n.bit_length() - 1
     pieces = CHUNKS + 2 + 3
@@ -390,15 +364,21 @@
     return pl.pallas_call(
         functools.partial(tree_kernel, n, levels),
         out_shape=[
+            jax.ShapeDtypeStruct(rhs.shape, BF16),
             jax.ShapeDtypeStruct(skel.shape, F32),
             jax.ShapeDtypeStruct((columns, node), BF16),
             jax.ShapeDtypeStruct((columns, node), F32),
         ],
-        in_specs=[hbm] * 6,
-        out_specs=[hbm, vmem, vmem],
+        in_specs=[pl.BlockSpec(memory_space=pltpu.SMEM)] * 2 + [hbm] * 7,
+        out_specs=[hbm, hbm, vmem, vmem],
         scratch_shapes=[
+            pltpu.VMEM(rhs.shape, BF16),
+            pltpu.VMEM(inverse.shape, BF16),
+            pltpu.VMEM(leaf_couple.shape, BF16),
+            pltpu.VMEM(rhs.shape, BF16),
+            pltpu.VMEM((cells * slots + 1, columns, width), F32),
+            pltpu.VMEM((4, blocks, columns, width), BF16),
             pltpu.VMEM((3, blocks, columns, width), BF16),
-            pltpu.VMEM((2, blocks // 2, columns, width), BF16),
             pltpu.VMEM((2, blocks // 2, columns, width), BF16),
             pltpu.VMEM((blocks, columns, width), F32),
             pltpu.VMEM(skel.shape, F32),
@@ -411,7 +391,8 @@
             pltpu.VMEM((levels, columns, node), BF16),
             pltpu.VMEM((levels, columns, node), BF16),
             pltpu.VMEM((levels, columns, node), BF16),
-            dma((4 + CHUNKS + 2,)),
+            dma((3, cells)),
+            dma((1 + CHUNKS + 2,)),
             dma((4, CHUNKS)),
             dma((4, CHUNKS)),
             dma((pieces,)), dma((pieces,)), dma((pieces,)),
@@ -423,7 +404,7 @@
         compiler_params=pltpu.CompilerParams(
             collective_id=0, has_side_effects=True, vmem_limit_bytes=60 * 2**20
         ),
-    )(send, own, skel, lift, mix, couple)
+    )(prev, last_of, rhs, inverse, leaf_couple, skel, lift, mix, couple)
 
 
 def on_device(
@@ -432,11 +413,20 @@
     position = lax.axis_index("cells")
     n = lax.axis_size("cells")
     columns, blocks, width = skeleton_in.shape
-    segments = skel_target.reshape(-1) - (position - HOP) * blocks
-    solved, own, send = leaf_call(segments, right_side, leaf_inverse, leaf_couple, blocks)
-    skel, node_solution, node_skeleton = tree_call(
-        n, send, own, skeleton_in.reshape(columns * blocks, width),
-        lift_ops[0], node_mix[0], node_couple[0],
+    targets = skel_target.reshape(-1) - (position - HOP) * blocks
+    total = targets.shape[0]
+    at = jnp.arange(total, dtype=jnp.int32)
+    rows = (2 * HOP + 1) * blocks
+
+    def latest(hit):
+        found = jnp.max(jnp.where(hit, at[None, :], -1), axis=1)
+        return jnp.where(found < 0, total, found)
+
+    prev = latest((targets[None, :] == targets[:, None]) & (at[None, :] < at[:, None]))
+    last_of = latest(targets[None, :] == jnp.arange(rows, dtype=jnp.int32)[:, None])
+    solved, skel, node_solution, node_skeleton = tree_call(
+        n, blocks, prev, last_of, right_side, leaf_inverse, leaf_couple,
+        skeleton_in.reshape(columns * blocks, width), lift_ops[0], node_mix[0], node_couple[0],
     )
     return (
         solved,

time: 99 us -> 86.2 us (0.87)
  the two profiles are of different devices: /device:TPU:11 before, /device:TPU:0 now
where the time goes in v3:
time: 86.2 us; the launch traced here: 84.7 us
  Pallas kernels  75.3 us (87%)
  local copies, waits for them, and re-layouts  6.67 us (8%)
  other arithmetic  2.05 us (2%)
    pallas_call x1, Pallas kernels, tree_call(): pl.pallas_call(functools.partial(tree_kernel, n, levels), out_shape=[jax....  75.3 us
    unnamed x8, local copies, waits for them, and re-layouts  6.59 us

profile of v3, /device:TPU:0, one launch (start us, length us, event | category | flops | bytes accessed | tf_op | source)
XLA Modules:
  0.0 84.7 jit_solution(18130232053369420923)
XLA Ops:
  0.6 0.7 broadcast_subtract_fusion
  1.3 0.1 sub.23
  1.4 0.2 select_reduce_fusion.1
  1.6 0.5 compare_select_fusion.1.prev
  2.1 0.1 select_reduce_fusion
  2.2 0.6 compare_select_fusion.last_of
  2.8 75.3 %shard_map.111 = (bf16[8,128,384]{2,1,0:T(8,128)(2,1)}, f32[4096,128]{1,0:T(8,128)}, bf16[128,512]{1,0:T(8,128)(2,1)}, f32[128,512]{1,0:T(8,128)}) custom-call(s32[72]{0:T(128)} %compare_select_fusion.1.prev, s32[160]{0:T(256)} %compare_select_fusion.last_of, bf16[8,128,384]{2,1,0:T(8,128)(2,1)} %rhs.1, bf16[8,384,384]{2,1,0:T(8,128)(2,1)} %inverse.1, ...), custom_call_target="tpu_custom_call" | custom-call | tf_op jit(solution)/shard_map/pallas_call | solution.py:364
  78.1 2.1 %copy.16 = bf16[8,128,384]{2,1,0:T(8,128)(2,1)} copy(bf16[8,128,384]{2,1,0:T(8,128)(2,1)} %get-tuple-element.16) | data formatting | bytes 1572864
  80.2 0.0 copy-start.1
  80.2 0.0 copy-start
  80.2 3.1 %copy.17 = f32[128,32,128]{2,1,0:T(8,128)} copy(f32[128,32,128]{2,1,0:T(8,128)} %bitcast.7) | data formatting | bytes 4194304
  83.3 0.0 copy-done.1
  83.3 0.7 copy.18
  84.0 0.0 copy-done
  84.0 0.7 copy.19
Async XLA Ops:
  80.2 3.1 %copy-start.1 = (bf16[128,512]{1,0:T(8,128)(2,1)S(1)}, bf16[128,512]{1,0:T(8,128)(2,1)}, u32[]{:S(2)}) copy-start(bf16[128,512]{1,0:T(8,128)(2,1)} %get-tuple-element.10) | copy-start | bytes 393220
  80.2 3.8 %copy-start = (f32[128,512]{1,0:T(8,128)S(1)}, f32[128,512]{1,0:T(8,128)}, u32[]{:S(2)}) copy-start(f32[128,512]{1,0:T(8,128)} %get-tuple-element.11) | copy-start | bytes 786436

commit v4 on v3

--- a/solution.py
+++ b/solution.py
@@ -18,11 +18,11 @@
 
 
 def tree_kernel(
-    n, levels, prev, last_of, rhs, inverse, leaf_couple, skel, lift, mix, couple,
+    n, levels, target, rhs, inverse, leaf_couple, skel, lift, mix, couple,
     out_leaf, out_skel, out_sol, out_node,
-    rhs_v, inverse_v, leaf_couple_v, leaf_v, partial, send, recv, relay, own_v, skel_v, flat, lift_g, mix_g, couple_g, mix_h, couple_h,
+    table_v, table, rhs_v, inverse_v, leaf_couple_v, leaf_v, partial, send, recv, relay, own_v, skel_v, flat, lift_g, mix_g, couple_g, mix_h, couple_h,
     mine, left_v, right_v,
-    leaf_sem, local_sem, port_send, port_recv, near_send, near_recv, far_send, far_recv, fwd_send, fwd_recv,
+    table_sem, leaf_sem, local_sem, port_send, port_recv, near_send, near_recv, far_send, far_recv, fwd_send, fwd_recv,
     half_send, half_recv, vec_send, vec_recv,
 ):
     me = lax.axis_index("cells")
@@ -58,6 +58,24 @@
         for copy in leaf_copies(c):
             copy.start()
 
+    total = cells * slots
+    lanes = table_v.shape[1]
+    lane = lax.broadcasted_iota(jnp.int32, (1, lanes), 1)
+    block = lane + (me - HOP) * blocks
+    names = [target[i // slots, i % slots] for i in range(total)]
+    named = jnp.full((1, lanes), -1, jnp.int32)
+    for i in range(total):
+        named = jnp.where(lane == i, names[i], named)
+    before = last = jnp.full((1, lanes), total, jnp.int32)
+    for i in range(total):
+        before = jnp.where(jnp.logical_and(named == names[i], lane > i), i, before)
+        last = jnp.where(block == names[i], i, last)
+    table_v[...] = jnp.zeros(table_v.shape, jnp.int32)
+    table_v[0:1, :] = before
+    table_v[1:2, :] = last
+    table_copy = pltpu.make_async_copy(table_v, table, table_sem)
+    table_copy.start()
+
     barrier = pltpu.get_barrier_semaphore()
     for step in partners:
         pl.semaphore_signal(barrier, inc=1, device_id=((me + step) % n, rank), device_id_type=MESH)
@@ -156,6 +174,8 @@
     def _(i):
         partial[i] = jnp.zeros((columns, width), F32)
 
+    table_copy.wait()
+
     @pl.loop(0, cells)
     def _(c):
         for copy in leaf_copies(c):
@@ -167,12 +187,12 @@
             update = dot(solved, jnp.concatenate([leaf_couple_v[c, j] for j in pair], axis=1))
             for at, j in enumerate(pair):
                 i = c * slots + j
-                partial[i] = update[:, at * width : (at + 1) * width] + partial[prev[i]]
+                partial[i] = update[:, at * width : (at + 1) * width] + partial[table[0, i]]
 
     def emit(role, q):
         @pl.loop(q * group, (q + 1) * group)
         def _(b):
-            send[role, b] = partial[last_of[row_of[role] * blocks + b]].astype(BF16)
+            send[role, b] = partial[table[1, row_of[role] * blocks + b]].astype(BF16)
 
     for at in range(first_half):
         for q in (at, at + first_half):
@@ -214,7 +234,7 @@
     for copy in locals_:
         copy.wait()
     for b in range(blocks):
-        own_v[b] = skel_v[pl.ds(b, columns, stride=blocks), :] - partial[last_of[HOP * blocks + b]]
+        own_v[b] = skel_v[pl.ds(b, columns, stride=blocks), :] - partial[table[1, HOP * blocks + b]]
 
     for at in range(2):
         role = (BEHIND, BESIDE)[at]
@@ -264,7 +284,10 @@
         for b in range(q * group, (q + 1) * group):
             arrived = recv[0, b].astype(F32) + recv[1, b].astype(F32) + recv[2, b].astype(F32)
             value = own_v[b] - arrived
-            skel_v[pl.ds(b, columns, stride=blocks), :] = value
+            if q < CHUNKS - 1:
+                skel_v[pl.ds(b, columns, stride=blocks), :] = value
+            else:
+                own_v[b] = value
             flat[:, b * width : (b + 1) * width] = value.astype(BF16)
         near_arrival(q).wait_recv()
         fwd_arrival(q).wait_recv()
@@ -278,8 +301,10 @@
     result = pltpu.make_async_copy(skel_v, out_skel, local_sem.at[0])
     sent = []
 
-    def merge(first, second, mixing, coupling):
-        solved = (dot(first, mixing[:node, :]) + dot(second, mixing[node:, :])).astype(BF16)
+    def merge(first, second, mixing, coupling, mixed=None):
+        if mixed is None:
+            mixed = dot(second, mixing[node:, :])
+        solved = (dot(first, mixing[:node, :]) + mixed).astype(BF16)
         skeleton = 0.5 * (first.astype(F32) + second.astype(F32)) - dot(solved, coupling[...])
         return solved, skeleton
 
@@ -293,20 +318,23 @@
             down.start()
             sent.append(down)
         else:
+            for b in range((CHUNKS - 1) * group, blocks):
+                skel_v[pl.ds(b, columns, stride=blocks), :] = own_v[b]
             result.start()
             for i in range(CHUNKS, count):
                 near_arrival(i).wait_recv()
                 fwd_arrival(i).wait_recv()
+            second = mine[0]
+            mixed = dot(second, mix_g[node:, :])
             for i in range(count, count + 2):
                 far_arrival(i).wait_recv()
                 forward(i).start()
-        up.wait_recv()
         if level > 0:
             down.wait_recv()
             second = right_v[level]
-        else:
-            second = mine[0]
-        _, skeleton = merge(left_v[level], second, mix_g, couple_g)
+            mixed = dot(second, mix_g[node:, :])
+        up.wait_recv()
+        _, skeleton = merge(left_v[level], second, mix_g, couple_g, mixed)
         mine[level + 1] = skeleton.astype(BF16)
 
     last = levels - 1
@@ -352,12 +380,13 @@
     leaf_out.wait()
 
 
-def tree_call(n, blocks, prev, last_of, rhs, inverse, leaf_couple, skel, lift, mix, couple):
+def tree_call(n, blocks, target, rhs, inverse, leaf_couple, skel, lift, mix, couple):
     cells, columns, _ = rhs.shape
     slots, width = leaf_couple.shape[1], leaf_couple.shape[3]
     node = couple.shape[0]
     levels = n.bit_length() - 1
     pieces = CHUNKS + 2 + 3
+    lanes = -(-max(cells * slots, (2 * HOP + 1) * blocks) // 128) * 128
     dma = pltpu.SemaphoreType.DMA
     vmem = pl.BlockSpec(memory_space=pltpu.VMEM)
     hbm = pl.BlockSpec(memory_space=pl.ANY)
@@ -369,9 +398,11 @@
             jax.ShapeDtypeStruct((columns, node), BF16),
             jax.ShapeDtypeStruct((columns, node), F32),
         ],
-        in_specs=[pl.BlockSpec(memory_space=pltpu.SMEM)] * 2 + [hbm] * 7,
+        in_specs=[pl.BlockSpec(memory_space=pltpu.SMEM)] + [hbm] * 7,
         out_specs=[hbm, hbm, vmem, vmem],
         scratch_shapes=[
+            pltpu.VMEM((8, lanes), jnp.int32),
+            pltpu.SMEM((8, lanes), jnp.int32),
             pltpu.VMEM(rhs.shape, BF16),
             pltpu.VMEM(inverse.shape, BF16),
             pltpu.VMEM(leaf_couple.shape, BF16),
@@ -391,6 +422,7 @@
             pltpu.VMEM((levels, columns, node), BF16),
             pltpu.VMEM((levels, columns, node), BF16),
             pltpu.VMEM((levels, columns, node), BF16),
+            dma,
             dma((3, cells)),
             dma((1 + CHUNKS + 2,)),
             dma((4, CHUNKS)),
@@ -404,29 +436,47 @@
         compiler_params=pltpu.CompilerParams(
             collective_id=0, has_side_effects=True, vmem_limit_bytes=60 * 2**20
         ),
-    )(prev, last_of, rhs, inverse, leaf_couple, skel, lift, mix, couple)
+    )(target, rhs, inverse, leaf_couple, skel, lift, mix, couple)
+
+
+def hand_out_kernel(cuts, *refs):
+    count = len(cuts)
+    sems = refs[-1]
+    copies = []
+    for src, dst, cut in zip(refs[:count], refs[count : 2 * count], cuts):
+        rows = src.shape[0] // cut
+        for i in range(cut):
+            part = pl.ds(i * rows, rows)
+            copies.append(pltpu.make_async_copy(src.at[part], dst.at[part], sems.at[len(copies)]))
+    for copy in copies:
+        copy.start()
+    for copy in copies:
+        copy.wait()
+
+
+def hand_out(*arrays):
+    cuts = (4, 8, 1, 2)
+    hbm = pl.BlockSpec(memory_space=pl.ANY)
+    return pl.pallas_call(
+        functools.partial(hand_out_kernel, cuts),
+        out_shape=[jax.ShapeDtypeStruct(a.shape, a.dtype) for a in arrays],
+        in_specs=[hbm] * len(arrays),
+        out_specs=[hbm] * len(arrays),
+        scratch_shapes=[pltpu.SemaphoreType.DMA((sum(cuts),))],
+        compiler_params=pltpu.CompilerParams(vmem_limit_bytes=60 * 2**20),
+    )(*arrays)
 
 
 def on_device(
     right_side, leaf_inverse, leaf_couple, skel_target, skeleton_in, lift_ops, node_mix, node_couple
 ):
-    position = lax.axis_index("cells")
     n = lax.axis_size("cells")
     columns, blocks, width = skeleton_in.shape
-    targets = skel_target.reshape(-1) - (position - HOP) * blocks
-    total = targets.shape[0]
-    at = jnp.arange(total, dtype=jnp.int32)
-    rows = (2 * HOP + 1) * blocks
-
-    def latest(hit):
-        found = jnp.max(jnp.where(hit, at[None, :], -1), axis=1)
-        return jnp.where(found < 0, total, found)
-
-    prev = latest((targets[None, :] == targets[:, None]) & (at[None, :] < at[:, None]))
-    last_of = latest(targets[None, :] == jnp.arange(rows, dtype=jnp.int32)[:, None])
-    solved, skel, node_solution, node_skeleton = tree_call(
-        n, blocks, prev, last_of, right_side, leaf_inverse, leaf_couple,
-        skeleton_in.reshape(columns * blocks, width), lift_ops[0], node_mix[0], node_couple[0],
+    solved, skel, node_solution, node_skeleton = hand_out(
+        *tree_call(
+            n, blocks, skel_target, right_side, leaf_inverse, leaf_couple,
+            skeleton_in.reshape(columns * blocks, width), lift_ops[0], node_mix[0], node_couple[0],
+        )
     )
     return (
         solved,

time: 86.2 us -> 176 us (2.04)
  Pallas kernels: 75.3 us -> 175 us
  local copies, waits for them, and re-layouts: 6.67 us -> 0 us
  other arithmetic: 2.05 us -> 0 us
    pallas_call x0 -> x1, Pallas kernels: none -> 101 us  [hand_out(): pl.pallas_call(functools.partial(hand_out_kernel, cuts), out_shape=[jax.S...]
    unnamed x8 -> x0, local copies, waits for them, and re-layouts: 6.59 us -> none
where the time goes in v4:
time: 176 us
  Pallas kernels  175 us (99%)
    pallas_call x1, Pallas kernels, hand_out(): pl.pallas_call(functools.partial(hand_out_kernel, cuts), out_shape=[jax.S...  101 us
    pallas_call x1, Pallas kernels, tree_call(): pl.pallas_call(functools.partial(tree_kernel, n, levels), out_shape=[jax....  74.9 us

profile of v4, /device:TPU:0, one launch (start us, length us, event | category | flops | bytes accessed | tf_op | source)
XLA Modules:
  0.0 176.1 jit_solution(11793323266300993977)
XLA Ops:
  0.6 74.9 %shard_map.111 = (bf16[8,128,384]{2,1,0:T(8,128)(2,1)}, f32[4096,128]{1,0:T(8,128)}, bf16[128,512]{1,0:T(8,128)(2,1)}, f32[128,512]{1,0:T(8,128)}) custom-call(s32[8,9]{1,0:T(8,128)} %target.1, bf16[8,128,384]{2,1,0:T(8,128)(2,1)} %rhs.1, bf16[8,384,384]{2,1,0:T(8,128)(2,1)} %inverse.1, bf16[8,9,384,128]{3,2,1,0:T(8,128)(2,1)} %leaf_couple.1, ...), custom_call_target="tpu_custom_call" | custom-call | tf_op jit(solution)/shard_map/pallas_call | solution.py:393
  75.6 100.5 %shard_map.112 = (bf16[8,128,384]{2,1,0:T(8,128)(2,1)}, f32[4096,128]{1,0:T(8,128)}, bf16[128,512]{1,0:T(8,128)(2,1)}, f32[128,512]{1,0:T(8,128)}) custom-call(bf16[8,128,384]{2,1,0:T(8,128)(2,1)} %get-tuple-element.12.refs_0_, f32[4096,128]{1,0:T(8,128)} %get-tuple-element.13.refs_1_, bf16[128,512]{1,0:T(8,128)(2,1)} %get-tuple-element.14.refs_2_, ...), custom_call_target="tpu_custom_call" | custom-call | tf_op jit(solution)/shard_map/pallas_call | solution.py:460

commit v5 on v4

--- a/solution.py
+++ b/solution.py
@@ -9,6 +9,7 @@
 
 HOP = 2
 CHUNKS = 4
+PIECES = 4
 MESH = pl.DeviceIdType.MESH
 F32, BF16 = jnp.float32, jnp.bfloat16
 
@@ -21,9 +22,9 @@
     n, levels, target, rhs, inverse, leaf_couple, skel, lift, mix, couple,
     out_leaf, out_skel, out_sol, out_node,
     table_v, table, rhs_v, inverse_v, leaf_couple_v, leaf_v, partial, send, recv, relay, own_v, skel_v, flat, lift_g, mix_g, couple_g, mix_h, couple_h,
-    mine, left_v, right_v,
+    mine, left_v, right_v, pair_v,
     table_sem, leaf_sem, local_sem, port_send, port_recv, near_send, near_recv, far_send, far_recv, fwd_send, fwd_recv,
-    half_send, half_recv, vec_send, vec_recv,
+    half_send, half_recv, vec_send, vec_recv, pair_send, pair_recv,
 ):
     me = lax.axis_index("cells")
     rank = lax.axis_index("rhs")
@@ -308,34 +309,57 @@
         skeleton = 0.5 * (first.astype(F32) + second.astype(F32)) - dot(solved, coupling[...])
         return solved, skeleton
 
-    for level in range(levels - 1):
+    def next_to(level, skeleton):
+        mine[level + 1] = skeleton.astype(BF16)
+
+    up = vector(mine.at[0], left_v.at[0], 0, 1)
+    up.start()
+    sent.append(up)
+    for b in range((CHUNKS - 1) * group, blocks):
+        skel_v[pl.ds(b, columns, stride=blocks), :] = own_v[b]
+    result.start()
+    for i in range(CHUNKS, count):
+        near_arrival(i).wait_recv()
+        fwd_arrival(i).wait_recv()
+    mixed = dot(mine[0], mix_g[node:, :])
+    for i in range(count, count + 2):
+        far_arrival(i).wait_recv()
+        forward(i).start()
+    up.wait_recv()
+    next_to(0, merge(left_v[0], mine[0], mix_g, couple_g, mixed)[1])
+
+    rows = columns // PIECES
+    parts = [pl.ds(i * rows, rows) for i in range(PIECES)]
+
+    def over(i):
+        return remote(mine.at[1, parts[i]], pair_v.at[0, parts[i]], pair_send.at[0, i], pair_recv.at[0, i], beside, rank)
+
+    def onward(i):
+        return remote(pair_v.at[0, parts[i]], pair_v.at[1, parts[i]], pair_send.at[1, i], pair_recv.at[1, i], behind, rank)
+
+    for i in range(PIECES):
+        over(i).start()
+    for i in range(PIECES):
+        over(i).wait_recv()
+        onward(i).start()
+    mixed = dot(pair_v[0], mix_g[pl.ds(pl.multiple_of((1 - odd) * node, node), node), :])
+    for i in range(PIECES):
+        onward(i).wait_recv()
+    solved = (mixed + dot(pair_v[1], mix_g[pl.ds(pl.multiple_of(odd * node, node), node), :])).astype(BF16)
+    skeleton = 0.5 * (pair_v[0].astype(F32) + pair_v[1].astype(F32)) - dot(solved, couple_g[...])
+    next_to(1, skeleton)
+
+    for level in range(2, levels - 1):
         d = reach[level]
         up = vector(mine.at[level], left_v.at[level], 2 * level, d)
         up.start()
-        sent.append(up)
-        if level > 0:
-            down = vector(mine.at[level], right_v.at[level], 2 * level + 1, -d)
-            down.start()
-            sent.append(down)
-        else:
-            for b in range((CHUNKS - 1) * group, blocks):
-                skel_v[pl.ds(b, columns, stride=blocks), :] = own_v[b]
-            result.start()
-            for i in range(CHUNKS, count):
-                near_arrival(i).wait_recv()
-                fwd_arrival(i).wait_recv()
-            second = mine[0]
-            mixed = dot(second, mix_g[node:, :])
-            for i in range(count, count + 2):
-                far_arrival(i).wait_recv()
-                forward(i).start()
-        if level > 0:
-            down.wait_recv()
-            second = right_v[level]
-            mixed = dot(second, mix_g[node:, :])
+        down = vector(mine.at[level], right_v.at[level], 2 * level + 1, -d)
+        down.start()
+        sent += [up, down]
+        down.wait_recv()
+        mixed = dot(right_v[level], mix_g[node:, :])
         up.wait_recv()
-        _, skeleton = merge(left_v[level], second, mix_g, couple_g, mixed)
-        mine[level + 1] = skeleton.astype(BF16)
+        next_to(level, merge(left_v[level], right_v[level], mix_g, couple_g, mixed)[1])
 
     last = levels - 1
     up = vector(mine.at[last], left_v.at[last], 2 * last, reach[last])
@@ -358,6 +382,9 @@
 
     for copy in sent:
         copy.wait_send()
+    for i in range(PIECES):
+        over(i).wait_send()
+        onward(i).wait_send()
     for i in range(count + len(halves)):
         to_near(i).wait_send()
         to_far(i).wait_send()
@@ -422,6 +449,7 @@
             pltpu.VMEM((levels, columns, node), BF16),
             pltpu.VMEM((levels, columns, node), BF16),
             pltpu.VMEM((levels, columns, node), BF16),
+            pltpu.VMEM((2, columns, node), BF16),
             dma,
             dma((3, cells)),
             dma((1 + CHUNKS + 2,)),
@@ -432,6 +460,8 @@
             dma((3,)), dma((3,)),
             dma((2 * levels,)),
             dma((2 * levels,)),
+            dma((2, PIECES)),
+            dma((2, PIECES)),
         ],
         compiler_params=pltpu.CompilerParams(
             collective_id=0, has_side_effects=True, vmem_limit_bytes=60 * 2**20
@@ -442,27 +472,32 @@
 def hand_out_kernel(cuts, *refs):
     count = len(cuts)
     sems = refs[-1]
-    copies = []
-    for src, dst, cut in zip(refs[:count], refs[count : 2 * count], cuts):
+    inward, outward = [], []
+    for src, dst, stage, cut in zip(refs[:count], refs[count : 2 * count], refs[2 * count : 3 * count], cuts):
         rows = src.shape[0] // cut
         for i in range(cut):
-            part = pl.ds(i * rows, rows)
-            copies.append(pltpu.make_async_copy(src.at[part], dst.at[part], sems.at[len(copies)]))
-    for copy in copies:
+            part, at = pl.ds(i * rows, rows), len(inward)
+            inward.append(pltpu.make_async_copy(src.at[part], stage.at[part], sems.at[0, at]))
+            outward.append(pltpu.make_async_copy(stage.at[part], dst.at[part], sems.at[1, at]))
+    for copy in inward:
         copy.start()
-    for copy in copies:
+    for copy, after in zip(inward, outward):
         copy.wait()
+        after.start()
+    for copy in outward:
+        copy.wait()
 
 
 def hand_out(*arrays):
-    cuts = (4, 8, 1, 2)
+    cuts = (2, 8, 1, 1)
     hbm = pl.BlockSpec(memory_space=pl.ANY)
     return pl.pallas_call(
         functools.partial(hand_out_kernel, cuts),
         out_shape=[jax.ShapeDtypeStruct(a.shape, a.dtype) for a in arrays],
         in_specs=[hbm] * len(arrays),
         out_specs=[hbm] * len(arrays),
-        scratch_shapes=[pltpu.SemaphoreType.DMA((sum(cuts),))],
+        scratch_shapes=[pltpu.VMEM(a.shape, a.dtype) for a in arrays]
+        + [pltpu.SemaphoreType.DMA((2, sum(cuts)))],
         compiler_params=pltpu.CompilerParams(vmem_limit_bytes=60 * 2**20),
     )(*arrays)
 

time: 176 us -> 82.3 us (0.47)
  Pallas kernels: 175 us -> 80.2 us
    pallas_call x1, Pallas kernels: 101 us -> 2.9 us  [hand_out(): pl.pallas_call(functools.partial(hand_out_kernel, cuts), out_shape=[jax.S...]
    pallas_call x1, Pallas kernels: 74.9 us -> 77.3 us  [tree_call(): pl.pallas_call(functools.partial(tree_kernel, n, levels), out_shape=[jax....]
where the time goes in v5:
time: 82.3 us; the launch traced here: 80.8 us
  Pallas kernels  80.2 us (97%)
    pallas_call x1, Pallas kernels, tree_call(): pl.pallas_call(functools.partial(tree_kernel, n, levels), out_shape=[jax....  77.3 us
    pallas_call x1, Pallas kernels, hand_out(): pl.pallas_call(functools.partial(hand_out_kernel, cuts), out_shape=[jax.S...  2.9 us

profile of v5, /device:TPU:0, one launch (start us, length us, event | category | flops | bytes accessed | tf_op | source)
XLA Modules:
  0.0 80.8 jit_solution(9699825784991301011)
XLA Ops:
  0.6 77.3 %shard_map.111 = (bf16[8,128,384]{2,1,0:T(8,128)(2,1)}, f32[4096,128]{1,0:T(8,128)}, bf16[128,512]{1,0:T(8,128)(2,1)}, f32[128,512]{1,0:T(8,128)}) custom-call(s32[8,9]{1,0:T(8,128)} %target.1, bf16[8,128,384]{2,1,0:T(8,128)(2,1)} %rhs.1, bf16[8,384,384]{2,1,0:T(8,128)(2,1)} %inverse.1, bf16[8,9,384,128]{3,2,1,0:T(8,128)(2,1)} %leaf_couple.1, ...), custom_call_target="tpu_custom_call" | custom-call | tf_op jit(solution)/shard_map/pallas_call | solution.py:420
  77.9 2.9 %shard_map.112 = (bf16[8,128,384]{2,1,0:T(8,128)(2,1)}, f32[4096,128]{1,0:T(8,128)}, bf16[128,512]{1,0:T(8,128)(2,1)}, f32[128,512]{1,0:T(8,128)}) custom-call(bf16[8,128,384]{2,1,0:T(8,128)(2,1)} %get-tuple-element.12.refs_0_, f32[4096,128]{1,0:T(8,128)} %get-tuple-element.13.refs_1_, bf16[128,512]{1,0:T(8,128)(2,1)} %get-tuple-element.14.refs_2_, ...), custom_call_target="tpu_custom_call" | custom-call | tf_op jit(solution)/shard_map/pallas_call | solution.py:494

commit v6 on v5

--- a/solution.py
+++ b/solution.py
@@ -9,7 +9,7 @@
 
 HOP = 2
 CHUNKS = 4
-PIECES = 4
+PARTS = 2
 MESH = pl.DeviceIdType.MESH
 F32, BF16 = jnp.float32, jnp.bfloat16
 
@@ -22,9 +22,9 @@
     n, levels, target, rhs, inverse, leaf_couple, skel, lift, mix, couple,
     out_leaf, out_skel, out_sol, out_node,
     table_v, table, rhs_v, inverse_v, leaf_couple_v, leaf_v, partial, send, recv, relay, own_v, skel_v, flat, lift_g, mix_g, couple_g, mix_h, couple_h,
-    mine, left_v, right_v, pair_v,
+    mine, left_v, right_v,
     table_sem, leaf_sem, local_sem, port_send, port_recv, near_send, near_recv, far_send, far_recv, fwd_send, fwd_recv,
-    half_send, half_recv, vec_send, vec_recv, pair_send, pair_recv,
+    half_send, half_recv, vec_send, vec_recv,
 ):
     me = lax.axis_index("cells")
     rank = lax.axis_index("rhs")
@@ -48,16 +48,15 @@
 
     cells, slots = leaf_couple.shape[0], leaf_couple.shape[1]
 
-    def leaf_copies(c):
-        return [
-            pltpu.make_async_copy(rhs.at[c], rhs_v.at[c], leaf_sem.at[0, c]),
-            pltpu.make_async_copy(inverse.at[c], inverse_v.at[c], leaf_sem.at[1, c]),
-            pltpu.make_async_copy(leaf_couple.at[c], leaf_couple_v.at[c], leaf_sem.at[2, c]),
-        ]
+    def leaf_copy(c, which):
+        src, dst = ((rhs, rhs_v), (inverse, inverse_v), (leaf_couple, leaf_couple_v))[which]
+        return pltpu.make_async_copy(src.at[c], dst.at[c], leaf_sem.at[which, c])
 
     for c in range(cells):
-        for copy in leaf_copies(c):
-            copy.start()
+        for which in range(2):
+            leaf_copy(c, which).start()
+    for c in range(cells):
+        leaf_copy(c, 2).start()
 
     total = cells * slots
     lanes = table_v.shape[1]
@@ -179,10 +178,14 @@
 
     @pl.loop(0, cells)
     def _(c):
-        for copy in leaf_copies(c):
-            copy.wait()
-        solved = dot(rhs_v[c], inverse_v[c]).astype(BF16)
-        leaf_v[c] = solved
+        for which in range(2):
+            leaf_copy(c, which).wait()
+        leaf_v[c] = dot(rhs_v[c], inverse_v[c]).astype(BF16)
+
+    @pl.loop(0, cells)
+    def _(c):
+        leaf_copy(c, 2).wait()
+        solved = leaf_v[c]
         for k in range(0, slots, 2):
             pair = [j for j in (k, k + 1) if j < slots]
             update = dot(solved, jnp.concatenate([leaf_couple_v[c, j] for j in pair], axis=1))
@@ -296,11 +299,22 @@
         total = part if total is None else total + part
     mine[0] = total.astype(BF16)
 
-    def vector(src, dst, at, step):
-        return remote(src, dst, vec_send.at[at], vec_recv.at[at], (me + step + n) % n, rank)
+    rows = columns // PARTS
+    parts = [pl.ds(h * rows, rows) for h in range(PARTS)]
+
+    def send_up(level, h):
+        return remote(
+            mine.at[level, parts[h]], left_v.at[level, parts[h]], vec_send.at[2 * level, h],
+            vec_recv.at[2 * level, h], (me + reach[level]) % n, rank,
+        )
+
+    def send_down(level, h):
+        return remote(
+            mine.at[level, parts[h]], right_v.at[level, parts[h]], vec_send.at[2 * level + 1, h],
+            vec_recv.at[2 * level + 1, h], (me - reach[level] + n) % n, rank,
+        )
 
     result = pltpu.make_async_copy(skel_v, out_skel, local_sem.at[0])
-    sent = []
 
     def merge(first, second, mixing, coupling, mixed=None):
         if mixed is None:
@@ -309,12 +323,13 @@
         skeleton = 0.5 * (first.astype(F32) + second.astype(F32)) - dot(solved, coupling[...])
         return solved, skeleton
 
-    def next_to(level, skeleton):
-        mine[level + 1] = skeleton.astype(BF16)
-
-    up = vector(mine.at[0], left_v.at[0], 0, 1)
-    up.start()
-    sent.append(up)
+    def next_to(level, h, skeleton):
+        mine[level + 1, parts[h]] = skeleton.astype(BF16)
+        send_up(level + 1, h).start()
+        send_down(level + 1, h).start()
+
+    for h in range(PARTS):
+        send_up(0, h).start()
     for b in range((CHUNKS - 1) * group, blocks):
         skel_v[pl.ds(b, columns, stride=blocks), :] = own_v[b]
     result.start()
@@ -325,66 +340,37 @@
     for i in range(count, count + 2):
         far_arrival(i).wait_recv()
         forward(i).start()
-    up.wait_recv()
-    next_to(0, merge(left_v[0], mine[0], mix_g, couple_g, mixed)[1])
-
-    rows = columns // PIECES
-    parts = [pl.ds(i * rows, rows) for i in range(PIECES)]
-
-    def over(i):
-        return remote(mine.at[1, parts[i]], pair_v.at[0, parts[i]], pair_send.at[0, i], pair_recv.at[0, i], beside, rank)
-
-    def onward(i):
-        return remote(pair_v.at[0, parts[i]], pair_v.at[1, parts[i]], pair_send.at[1, i], pair_recv.at[1, i], behind, rank)
-
-    for i in range(PIECES):
-        over(i).start()
-    for i in range(PIECES):
-        over(i).wait_recv()
-        onward(i).start()
-    mixed = dot(pair_v[0], mix_g[pl.ds(pl.multiple_of((1 - odd) * node, node), node), :])
-    for i in range(PIECES):
-        onward(i).wait_recv()
-    solved = (mixed + dot(pair_v[1], mix_g[pl.ds(pl.multiple_of(odd * node, node), node), :])).astype(BF16)
-    skeleton = 0.5 * (pair_v[0].astype(F32) + pair_v[1].astype(F32)) - dot(solved, couple_g[...])
-    next_to(1, skeleton)
-
-    for level in range(2, levels - 1):
-        d = reach[level]
-        up = vector(mine.at[level], left_v.at[level], 2 * level, d)
-        up.start()
-        down = vector(mine.at[level], right_v.at[level], 2 * level + 1, -d)
-        down.start()
-        sent += [up, down]
-        down.wait_recv()
-        mixed = dot(right_v[level], mix_g[node:, :])
-        up.wait_recv()
-        next_to(level, merge(left_v[level], right_v[level], mix_g, couple_g, mixed)[1])
+    for h in range(PARTS):
+        send_up(0, h).wait_recv()
+        part = mixed[h * rows : (h + 1) * rows]
+        next_to(0, h, merge(left_v[0, parts[h]], mine[0, parts[h]], mix_g, couple_g, part)[1])
+    pass_on(2)
+
+    for level in range(1, levels - 1):
+        for h in range(PARTS):
+            send_down(level, h).wait_recv()
+            send_up(level, h).wait_recv()
+            next_to(level, h, merge(left_v[level, parts[h]], right_v[level, parts[h]], mix_g, couple_g)[1])
 
     last = levels - 1
-    up = vector(mine.at[last], left_v.at[last], 2 * last, reach[last])
-    down = vector(mine.at[last], right_v.at[last], 2 * last + 1, -reach[last])
-    up.start()
-    down.start()
-    sent += [up, down]
-    pass_on(2)
     far_arrival(count + 2).wait_recv()
     forward(count + 2).start()
-    up.wait_recv()
-    down.wait_recv()
     for i in range(count, count + len(halves)):
         near_arrival(i).wait_recv()
         fwd_arrival(i).wait_recv()
-    solved, skeleton = merge(right_v[last], left_v[last], mix_h, couple_h)
-    solved, skeleton = merge(skeleton.astype(BF16), solved, mix_g, couple_g)
-    out_sol[...] = solved
-    out_node[...] = skeleton
-
-    for copy in sent:
-        copy.wait_send()
-    for i in range(PIECES):
-        over(i).wait_send()
-        onward(i).wait_send()
+    for h in range(PARTS):
+        send_down(last, h).wait_recv()
+        send_up(last, h).wait_recv()
+        solved, skeleton = merge(right_v[last, parts[h]], left_v[last, parts[h]], mix_h, couple_h)
+        solved, skeleton = merge(skeleton.astype(BF16), solved, mix_g, couple_g)
+        out_sol[parts[h], :] = solved
+        out_node[parts[h], :] = skeleton
+
+    for level in range(levels):
+        for h in range(PARTS):
+            send_up(level, h).wait_send()
+            if level > 0:
+                send_down(level, h).wait_send()
     for i in range(count + len(halves)):
         to_near(i).wait_send()
         to_far(i).wait_send()
@@ -449,7 +435,6 @@
             pltpu.VMEM((levels, columns, node), BF16),
             pltpu.VMEM((levels, columns, node), BF16),
             pltpu.VMEM((levels, columns, node), BF16),
-            pltpu.VMEM((2, columns, node), BF16),
             dma,
             dma((3, cells)),
             dma((1 + CHUNKS + 2,)),
@@ -458,10 +443,8 @@
             dma((pieces,)), dma((pieces,)), dma((pieces,)),
             dma((pieces,)), dma((pieces,)), dma((pieces,)),
             dma((3,)), dma((3,)),
-            dma((2 * levels,)),
-            dma((2 * levels,)),
-            dma((2, PIECES)),
-            dma((2, PIECES)),
+            dma((2 * levels, PARTS)),
+            dma((2 * levels, PARTS)),
         ],
         compiler_params=pltpu.CompilerParams(
             collective_id=0, has_side_effects=True, vmem_limit_bytes=60 * 2**20

time: 82.3 us -> 78.5 us (0.954); the launches traced: 80.8 us -> 78.3 us
  Pallas kernels: 80.2 us -> 77.7 us
    pallas_call x1, Pallas kernels: 77.3 us -> 74.8 us  [tree_call(): pl.pallas_call(functools.partial(tree_kernel, n, levels), out_shape=[jax....]
where the time goes in v6:
time: 78.5 us; the launch traced here: 78.3 us
  Pallas kernels  77.7 us (99%)
    pallas_call x1, Pallas kernels, tree_call(): pl.pallas_call(functools.partial(tree_kernel, n, levels), out_shape=[jax....  74.8 us
    pallas_call x1, Pallas kernels, hand_out(): pl.pallas_call(functools.partial(hand_out_kernel, cuts), out_shape=[jax.S...  2.9 us

profile of v6, /device:TPU:0, one launch (start us, length us, event | category | flops | bytes accessed | tf_op | source)
XLA Modules:
  0.0 78.3 jit_solution(16040865901890136360)
XLA Ops:
  0.6 74.8 %shard_map.111 = (bf16[8,128,384]{2,1,0:T(8,128)(2,1)}, f32[4096,128]{1,0:T(8,128)}, bf16[128,512]{1,0:T(8,128)(2,1)}, f32[128,512]{1,0:T(8,128)}) custom-call(s32[8,9]{1,0:T(8,128)} %target.1, bf16[8,128,384]{2,1,0:T(8,128)(2,1)} %rhs.1, bf16[8,384,384]{2,1,0:T(8,128)(2,1)} %inverse.1, bf16[8,9,384,128]{3,2,1,0:T(8,128)(2,1)} %leaf_couple.1, ...), custom_call_target="tpu_custom_call" | custom-call | tf_op jit(solution)/shard_map/pallas_call | solution.py:406
  75.4 2.9 %shard_map.112 = (bf16[8,128,384]{2,1,0:T(8,128)(2,1)}, f32[4096,128]{1,0:T(8,128)}, bf16[128,512]{1,0:T(8,128)(2,1)}, f32[128,512]{1,0:T(8,128)}) custom-call(bf16[8,128,384]{2,1,0:T(8,128)(2,1)} %get-tuple-element.12.refs_0_, f32[4096,128]{1,0:T(8,128)} %get-tuple-element.13.refs_1_, bf16[128,512]{1,0:T(8,128)(2,1)} %get-tuple-element.14.refs_2_, ...), custom_call_target="tpu_custom_call" | custom-call | tf_op jit(solution)/shard_map/pallas_call | solution.py:477
